TPU v7x, 256 devices: a whole 4x4x8 slice. The times are simulated.
256 devices in a mesh: ctx: 64 (over y, z, x_lo), head: 4 (over x_hi, core).
Axes of the slice: x: 4 (x_hi: 2, x_lo: 2; x = x_hi * 2 + x_lo), y: 4, z: 8, core: 2. Of those that a mesh axis runs over, the one named last changes fastest.
Arguments:
- queries: bfloat16 [512, 64, 128], P('ctx', 'head'), may hold values from -120 to 120
- cache_keys: bfloat16 [16384, 4, 128], P('ctx', 'head'), may hold values from -5 to 5
- stored_cache_values: bfloat16 [16384, 4, 128], P('ctx', 'head'), may hold values from -5 to 5
- turn_keys: bfloat16 [512, 4, 128], P('ctx', 'head'), may hold values from -5 to 5
- turn_values: bfloat16 [512, 4, 128], P('ctx', 'head'), may hold values from -5 to 5
- block_mask: int32 [4, 128], replicated, may hold values from 0 to 1, as said below
- doc_ids: int32 [512], replicated, may hold values from 0 to 7, never falling along the last dimension, each value on 1 to 256 neighbouring positions
- slot_ids: int32 [128], replicated, may hold values from 0 to 255, as said below
- out_weight: bfloat16 [8192, 16384], P('head', 'ctx'), may hold values from -0.0625 to 0.0625
Outputs:
- layer_out: float32 [512, 16384], P('head', 'ctx')
- append_slot_keys: bfloat16 [1024, 4, 128], P('ctx', 'head')
- append_slot_values: bfloat16 [1024, 4, 128], P('ctx', 'head')
Inputs may be any that keep to these rules, and one draw needn't show every extreme that they name: `block_mask`: column 0 and the last two columns are 1 in every row. `slot_ids`: distinct; piece p is kept by ctx index slot_ids[p] // 4 in its slot slot_ids[p] % 4. `doc_ids`: never falling along the new turn.
All inputs are finite; a program needn't handle non-finite values.
Results may differ from a plain program's by a relative error of at most 0.012.
Values may be sent and summed in bfloat16 or wider, within the bound.
A program may use at most 64 MiB of HBM per device.

v0:
```python
import math

import jax
import jax.numpy as jnp
from jax import lax
from jax.sharding import PartitionSpec as P

BLK = 128
SLOTS = 4


NEG_FILL = -1e30


def attend(query_rows, key_rows, value_rows, allowed):
    row_count = query_rows.shape[0]
    kv_heads = key_rows.shape[1]
    head_width = query_rows.shape[2]
    group_size = query_rows.shape[1] // kv_heads
    grouped = query_rows.reshape(row_count, kv_heads, group_size, head_width)
    scores = jnp.einsum("nkgd,mkd->nkgm", grouped, key_rows, preferred_element_type=jnp.float32) * (
        1.0 / math.sqrt(head_width)
    )
    mask_four = allowed[:, None, None, :]
    peak_score = jnp.max(jnp.where(mask_four, scores, NEG_FILL), axis=-1)
    softmax_terms = jnp.where(mask_four, jnp.exp(scores - peak_score[..., None]), 0.0)
    weight_sum = jnp.sum(softmax_terms, axis=-1)
    weights = softmax_terms.astype(jnp.bfloat16)
    output = jnp.einsum("nkgm,mkd->nkgd", weights, value_rows, preferred_element_type=jnp.float32)
    return (peak_score, weight_sum, output)


def on_device(
    queries,
    cache_keys,
    stored_cache_values,
    turn_keys,
    turn_values,
    block_mask,
    doc_ids,
    slot_ids,
    out_weight,
):
    loop_size = lax.axis_size("ctx")
    my_index = lax.axis_index("ctx")
    rows_dev = queries.shape[0]
    total_rows = rows_dev * loop_size
    cache_dev = cache_keys.shape[0]
    kv_heads = cache_keys.shape[1]
    head_width = cache_keys.shape[2]
    group_size = queries.shape[1] // kv_heads
    piece_count = 2 * loop_size
    piece_rows = total_rows // piece_count
    slot_count = SLOTS
    all_keys, all_values = (
        lax.all_gather(turn_keys, "ctx", axis=0, tiled=True),
        lax.all_gather(turn_values, "ctx", axis=0, tiled=True),
    )
    slot_numbers = my_index * slot_count + jnp.arange(slot_count, dtype=jnp.int32)
    select = slot_ids[None, :] == slot_numbers[:, None]
    picker_function = select.astype(jnp.bfloat16)
    flattened_width = piece_rows * kv_heads * head_width
    append_slot_keys = (
        jnp.dot(
            picker_function,
            all_keys.reshape(piece_count, flattened_width),
            preferred_element_type=jnp.float32,
        )
        .astype(jnp.bfloat16)
        .reshape(slot_count * piece_rows, kv_heads, head_width)
    )
    append_slot_values = (
        jnp.dot(
            picker_function,
            all_values.reshape(piece_count, flattened_width),
            preferred_element_type=jnp.float32,
        )
        .astype(jnp.bfloat16)
        .reshape(slot_count * piece_rows, kv_heads, head_width)
    )
    piece_numbers = jnp.arange(piece_count, dtype=jnp.int32)
    slot_piece = jnp.sum(jnp.where(select, piece_numbers[None, :], 0), axis=1)
    slot_live = jnp.any(select, axis=1)
    within = jnp.arange(piece_rows, dtype=jnp.int32)
    new_pos = (slot_piece[:, None] * piece_rows + within[None, :]).reshape(-1)
    new_live = jnp.repeat(slot_live, piece_rows)
    doc_pieces = doc_ids.reshape(piece_count, piece_rows)
    new_docs = jnp.sum(jnp.where(select[:, :, None], doc_pieces[None, :, :], 0), axis=1).reshape(-1)
    local_keys = jnp.concatenate([cache_keys, append_slot_keys], axis=0)
    local_values = jnp.concatenate([stored_cache_values, append_slot_values], axis=0)
    my_columns = lax.dynamic_slice_in_dim(
        block_mask, my_index * (cache_dev // BLK), cache_dev // BLK, 1
    )
    cache_allowed = jnp.repeat(jnp.repeat(my_columns, BLK, axis=0), BLK, axis=1) == 1

    def local_mask(offset, row_count):
        positions = offset + jnp.arange(row_count, dtype=jnp.int32)
        new_part = (
            new_live[None, :]
            & (new_pos[None, :] <= positions[:, None])
            & (new_docs[None, :] == doc_ids[:, None])
        )
        return jnp.concatenate([cache_allowed, new_part], axis=1)

    reduced_shape = (rows_dev, kv_heads, group_size)
    everyone = lax.all_gather(queries, "ctx", axis=0, tiled=True)
    block_rows = math.gcd(total_rows, 512)

    def one_block(block_index):
        offset = block_index * block_rows
        return attend(everyone, local_keys, local_values, local_mask(offset, block_rows))

    peak_blocks, sum_blocks, out_blocks = lax.map(
        one_block, jnp.arange(total_rows // block_rows, dtype=jnp.int32)
    )
    peak_flat = peak_blocks.reshape((total_rows,) + peak_blocks.shape[2:])
    sum_flat = sum_blocks.reshape((total_rows,) + sum_blocks.shape[2:])
    out_flat = out_blocks.reshape((total_rows,) + out_blocks.shape[2:])
    peak_back, sum_back, out_back = (
        lax.all_to_all(peak_flat, "ctx", split_axis=0, concat_axis=0, tiled=True),
        lax.all_to_all(sum_flat, "ctx", split_axis=0, concat_axis=0, tiled=True),
        lax.all_to_all(out_flat, "ctx", split_axis=0, concat_axis=0, tiled=True),
    )
    peaks = peak_back.reshape((loop_size,) + reduced_shape)
    sums = sum_back.reshape((loop_size,) + reduced_shape)
    outs = out_back.reshape((loop_size,) + reduced_shape + (head_width,))
    new_peak = jnp.max(peaks, axis=0)
    scales = jnp.exp(peaks - new_peak[None])
    weight_sum = jnp.sum(sums * scales, axis=0)
    output = jnp.sum(outs * scales[..., None], axis=0)
    attended = (
        (output / weight_sum[..., None])
        .astype(jnp.bfloat16)
        .reshape(rows_dev, kv_heads * group_size * head_width)
    )
    terms = jnp.dot(
        lax.all_gather(attended, "ctx", axis=0, tiled=True),
        out_weight,
        preferred_element_type=jnp.float32,
    )
    layer_out = lax.psum_scatter(terms, "head", scatter_dimension=0, tiled=True)
    return (layer_out, append_slot_keys, append_slot_values)


def solution(mesh):
    placed = (
        P("ctx", "head", None),
        P("ctx", "head", None),
        P("ctx", "head", None),
        P("ctx", "head", None),
        P("ctx", "head", None),
        P(),
        P(),
        P(),
        P("head", "ctx"),
    )
    return jax.shard_map(
        on_device,
        mesh=mesh,
        in_specs=placed,
        out_specs=(P("head", "ctx"), P("ctx", "head", None), P("ctx", "head", None)),
        check_vma=False,
    )
```

profile of v0, /device:TPU:1, one launch (start us, length us, event | category | flops | bytes accessed | tf_op | source)
XLA Modules:
  0.0 774.4 jit_solution(7021717944092997897)
XLA Ops:
  7.2 0.0 copy-start
  7.2 0.0 all-gather.3.cloned.1.call-start
  7.2 1.5 copy.25
  8.7 0.0 all-gather.3.cloned.1.call-update
  8.7 0.8 dynamic-slice_compare_fusion
  9.5 0.1 copy.23
  9.6 0.8 fusion.28
  10.4 0.1 broadcast_in_dim.94
  10.5 0.1 and.19
  10.6 0.1 broadcast_bitcast_fusion
  10.7 0.1 select_reduce_fusion.1
  10.8 0.1 iota_add_fusion
  10.9 0.1 add.48
  11.0 0.8 broadcast_in_dim.98
  11.8 0.1 copy.24
  11.8 0.2 select_reduce_fusion
  12.0 0.1 eq.60
  12.1 134.6 %all_gather.13 = bf16[512,1,128]{2,0,1:T(8,128)(2,1)S(1)} all-gather(bf16[8,1,128]{2,0,1:T(8,128)(2,1)} %param.12), channel_id=1, replica_groups=mesh['ctx'=64,'head'=4] {'ctx'}, dimensions={0}, use_global_device_ids=true | all-gather | bytes 133120 | tf_op jit(solution)/shard_map/all_gather | solution.py:56
  146.7 0.1 reshape.197
  146.8 0.1 convolution_convert_fusion
  146.9 124.7 %all_gather.12 = bf16[512,1,128]{2,0,1:T(8,128)(2,1)S(1)} all-gather(bf16[8,1,128]{2,0,1:T(8,128)(2,1)} %param.13), channel_id=1, replica_groups=mesh['ctx'=64,'head'=4] {'ctx'}, dimensions={0}, use_global_device_ids=true | all-gather | bytes 133120 | tf_op jit(solution)/shard_map/all_gather | solution.py:57
  271.6 0.1 reshape.194
  271.7 0.8 fusion.23
  272.5 0.0 copy-start.2
  272.5 0.0 all-gather.3.cloned.1.call-done
  272.6 3.2 fusion
  275.8 0.0 copy-start.1
  275.8 3.4 copy-done.1
  279.2 1.9 fusion.3
  281.0 0.0 copy-done.3
  281.1 0.5 broadcast.107
  281.6 0.6 reduce.7
  282.2 0.1 copy.36
  282.3 0.8 reshape.209
  283.1 4.6 all-to-all-start.2
  287.7 0.1 convolution_convert_fusion.1
  287.8 0.6 reduce.5
  288.4 0.1 copy.35
  288.6 0.8 reshape.207
  289.3 7.6 all-to-all-done.2
  296.9 4.6 all-to-all-start.1
  301.5 0.0 copy-done.2
  301.5 7.9 %fusion.12 = f32[512,1,16,128]{0,3,2,1:T(8,128)} fusion(f32[272,512,16]{1,0,2:T(8,128)} %copy-done.1, f32[512,16]{0,1:T(8,128)S(1)} %get-tuple-element.29, pred[512,272]{0,1:T(8,128)(4,1)S(1)} %pad_add_fusion, bf16[16,1,128]{2,0,1:T(8,128)(2,1)S(1)} %reshape.195, bf16[256,1,128]{2,0,1:T(8,128)(2,1)S(1)} %copy-done.2), kind=kOutput, calls=%fused_computation.14 | convolution fusion | flops 579477504 | bytes 13348864 | tf_op jit(solution)/shard_map/while/body/eval_jaxpr/nkgm,mkd->nkgd/dot_general | solution.py:29
  309.4 5.4 copy.26
  314.9 0.0 copy-done.4
  314.9 0.0 all-to-all-done.1
  314.9 10.9 %all-to-all-start = ((f32[512,1,16,128]{3,2,1,0:T(8,128)}), f32[512,1,16,128]{3,2,1,0:T(8,128)}, u32[]{:S(2)}, u32[]{:S(2)}) async-start(f32[512,1,16,128]{3,2,1,0:T(8,128)} %copy.26), calls=%async_computation | async-start | bytes 8388608 | tf_op jit(solution)/shard_map/all_to_all | solution.py:122
  325.8 0.0 all-gather.5.cloned.1.call-start
  325.9 0.7 reduce.8
  326.6 0.5 reshape.210
  327.1 0.7 reduce.6
  327.8 0.5 reshape.208
  328.2 0.1 bitcast_reduce_fusion
  328.3 0.1 multiply_reduce_fusion.1
  328.4 49.3 %all-to-all-done = f32[512,1,16,128]{3,2,1,0:T(8,128)} async-done(((f32[512,1,16,128]{3,2,1,0:T(8,128)}), f32[512,1,16,128]{3,2,1,0:T(8,128)}, u32[]{:S(2)}, u32[]{:S(2)}) %all-to-all-start) | async-done | bytes 4194336 | tf_op jit(solution)/shard_map/all_to_all | solution.py:122
  377.8 2.8 multiply_reduce_fusion
  380.6 0.1 fusion.21
  380.7 0.6 copy.33
  381.3 0.0 all-gather.5.cloned.1.call-update
  381.3 0.0 reduce-scatter.2.cloned.1.call-start
  381.4 308.5 %all-gather.5.cloned.1.call-done = bf16[512,2048]{1,0:T(8,128)(2,1)} async-done(((bf16[8,2048]{1,0:T(8,128)(2,1)}), bf16[512,2048]{1,0:T(8,128)(2,1)}) %all-gather.5.cloned.1.call-update) | async-done | bytes 2097168 | tf_op jit(solution)/shard_map/all_gather | solution.py:137
  689.9 3.1 fusion.29
  693.0 0.0 reduce-scatter.2.cloned.1.call-update
  693.0 74.8 %reduce-scatter.2.cloned.1.call-done = f32[128,256]{1,0:T(8,128)} async-done(((f32[512,256]{1,0:T(8,128)}), f32[128,256]{1,0:T(8,128)}) %reduce-scatter.2.cloned.1.call-update) | async-done | bytes 131088 | tf_op jit(solution)/shard_map/reduce_scatter | solution.py:141
  (11 shorter events, 0.1 us)
Async XLA Ops:
  7.2 682.7 %copy-start = (bf16[2048,256]{1,0:T(8,128)(2,1)S(1)}, bf16[2048,256]{1,0:T(8,128)(2,1)}, u32[]{:S(2)}) copy-start(bf16[2048,256]{1,0:T(8,128)(2,1)} %param.17) | copy-start | bytes 3145732
  7.2 265.4 %all-gather.3.cloned.1.call-start = ((), (), s32[]{:S(2)}) async-start(), calls=%async_computation.4 | async-start | bytes 2129920 | tf_op jit(solution)/shard_map/all_gather | solution.py:106
  146.9 134.1 %copy-start.3 = (bf16[16,1,128]{2,0,1:T(8,128)(2,1)}, bf16[16,1,128]{2,0,1:T(8,128)(2,1)S(1)}, u32[]{:S(2)}) copy-start(bf16[16,1,128]{2,0,1:T(8,128)(2,1)S(1)} %reshape.198) | copy-start | bytes 12292
  272.5 29.0 %copy-start.2 = (bf16[256,1,128]{2,0,1:T(8,128)(2,1)S(1)}, bf16[256,1,128]{2,0,1:T(8,128)(2,1)}, u32[]{:S(2)}) copy-start(bf16[256,1,128]{2,0,1:T(8,128)(2,1)} %param.11) | copy-start | bytes 196612
  275.8 3.4 copy-start.1
  283.1 13.8 %all-to-all-start.2 = ((f32[64,1,128]{2,1,0:T(1,128)}), f32[64,1,128]{2,1,0:T(1,128)S(1)}, u32[]{:S(2)}, u32[]{:S(2)}) async-start(f32[64,1,128]{2,1,0:T(1,128)} %reshape.209), calls=%async_computation.2 | async-start | bytes 65536 | tf_op jit(solution)/shard_map/all_to_all | solution.py:121
  287.8 27.1 %copy-start.4 = (bf16[16,1,128]{2,0,1:T(8,128)(2,1)}, bf16[16,1,128]{2,0,1:T(8,128)(2,1)S(1)}, u32[]{:S(2)}) copy-start(bf16[16,1,128]{2,0,1:T(8,128)(2,1)S(1)} %reshape.195) | copy-start | bytes 12292
  296.9 17.9 %all-to-all-start.1 = ((f32[64,1,128]{2,1,0:T(1,128)}), f32[64,1,128]{2,1,0:T(1,128)S(1)}, u32[]{:S(2)}, u32[]{:S(2)}) async-start(f32[64,1,128]{2,1,0:T(1,128)} %reshape.207), calls=%async_computation.1 | async-start | bytes 65536 | tf_op jit(solution)/shard_map/all_to_all | solution.py:120
  314.9 62.9 %all-to-all-start = ((f32[512,1,16,128]{3,2,1,0:T(8,128)}), f32[512,1,16,128]{3,2,1,0:T(8,128)}, u32[]{:S(2)}, u32[]{:S(2)}) async-start(f32[512,1,16,128]{3,2,1,0:T(8,128)} %copy.26), calls=%async_computation | async-start | bytes 8388608 | tf_op jit(solution)/shard_map/all_to_all | solution.py:122
  325.8 364.1 %all-gather.5.cloned.1.call-start = ((), (), s32[]{:S(2)}) async-start(), calls=%async_computation.5 | async-start | bytes 2129920 | tf_op jit(solution)/shard_map/all_gather | solution.py:137
  381.3 386.5 %reduce-scatter.2.cloned.1.call-start = ((), (), s32[]{:S(2)}) async-start(), calls=%async_computation.6 | async-start | bytes 655360 | tf_op jit(solution)/shard_map/reduce_scatter | solution.py:141
Sparse Core Ops, SparseCore 0:
  10.3 204.7 all-gather.2
  381.5 308.3 all-gather.4
  693.2 74.6 reduce-scatter.1
where the time goes:
time: 775 us; the launch traced here: 774 us
  waiting for transfers between devices  440 us (57%)
  blocking collectives  259 us (33%)
  starting transfers between devices  20.2 us (3%)
  local copies, waits for them, and re-layouts  15.9 us (2%)
  matrix products  14.4 us (2%)
  between operations  14 us (2%)
  other arithmetic  10.3 us (1%)
    all_gather x1, waiting for transfers between devices, on_device(): lax.all_gather(attended, 'ctx', axis=0, tiled=True)  309 us
    all_gather x1, blocking collectives, on_device(): lax.all_gather(turn_keys, 'ctx', axis=0, tiled=True)  135 us
    all_gather x1, blocking collectives, on_device(): lax.all_gather(turn_values, 'ctx', axis=0, tiled=True)  125 us
    reduce_scatter x1, waiting for transfers between devices, on_device(): layer_out = lax.psum_scatter(terms, 'head', scatter_dimension=0, tiled=True)  74.8 us
    all_to_all x1, waiting for transfers between devices, on_device(): lax.all_to_all(out_flat, 'ctx', split_axis=0, concat_axis=0, tiled=True)  49.3 us
  transfers between devices with their start and end apart: 6, of which 4 were waited for; matrix products, arithmetic and copies ran while one was open for 3% of the time, Pallas kernels for 0%

commit v1 on v0

v1 whole, which is shorter than its diff:
```python
import math

import jax
import jax.numpy as jnp
from jax import lax
from jax.experimental import pallas as pl
from jax.experimental.pallas import tpu as pltpu
from jax.sharding import PartitionSpec as P

MESH = pl.DeviceIdType.MESH
F32 = jnp.float32
BF16 = jnp.bfloat16

NY, NZ, NX = 4, 8, 2
NYX = NY * NX
HEAD = 128
KEYS = 256
GROUP = 16
ROWS = 8
NEG = -1e30
FLOOR = -1e29
SCALE = math.log2(math.e) / math.sqrt(HEAD)

YX = [(0, 0), (0, 1), (1, 0), (3, 0), (1, 1), (3, 1), (2, 0), (2, 1)]
PAIRS = [YX[0:2], YX[2:4], YX[4:6], YX[6:8]]


def nt(a, b):
    return lax.dot_general(a, b, (((1,), (1,)), ((), ())), preferred_element_type=F32)


def mm(a, b):
    return jnp.dot(a, b, preferred_element_type=F32)


def iota(shape, dim):
    return lax.broadcasted_iota(jnp.int32, shape, dim)


def kernel(
    q_in, ck_in, cv_in, w_in, tk_ref, tv_ref, doc_ref, slot_ref, mask_ref,
    out_ref, ak_ref, av_ref,
    q_raw, q_send, q_all, k_all, v_all, vt_all, w_all, turn,
    peak, acc, o_send, st_send, o_recv, st_recv, part_a, part_b, terms, h_send, h_recv, x_recv,
    sem_in, sem_q, sem_kv, sem_t, sem_tt, sem_rs, sem_a1, sem_b1, sem_a2, sem_b2, sem_h,
):
    c = lax.axis_index("ctx")
    h = lax.axis_index("head")
    y, z, x = c // (NZ * NX), (c // NX) % NZ, c % NX
    xh, core = h // 2, h % 2
    yx = y * NX + x

    def dev(dy=0, dz=0, dx=0, dxh=0, dcore=0):
        ty, tz, tx = (y + dy) % NY, (z + dz) % NZ, (x + dx) % NX
        return ((ty * NZ + tz) * NX + tx, (xh + dxh) % 2 * 2 + (core + dcore) % 2)

    def send(src, dst, sems, i, device):
        copy = pltpu.make_async_remote_copy(
            src_ref=src, dst_ref=dst, send_sem=sems.at[0, i], recv_sem=sems.at[1, i],
            device_id=device, device_id_type=MESH,
        )
        copy.start()
        return copy

    def fetch(src, dst, i):
        copy = pltpu.make_async_copy(src, dst, sem_in.at[i])
        copy.start()
        return copy

    get_q = fetch(q_in, q_raw, 0)
    get_k = fetch(ck_in, k_all.at[0], 1)
    get_v = fetch(cv_in, v_all.at[0], 2)
    get_w = fetch(w_in, w_all, 3)

    barrier = pltpu.get_barrier_semaphore()
    peers = [dict(dz=d) for d in range(1, NZ)]
    peers += [dict(dy=dy, dx=dx) for dy, dx in YX[1:]]
    peers += [dict(dcore=1), dict(dxh=1)]
    for p in peers:
        pl.semaphore_signal(barrier, inc=1, device_id=dev(**p), device_id_type=MESH)

    turn[z, yx] = jnp.concatenate(
        [tk_ref[...].astype(F32), tv_ref[...].astype(F32)], axis=0
    ).astype(BF16)
    get_q.wait()
    i0, i1 = iota((128, 128), 0), iota((128, 128), 1)
    order = (i1 == (i0 % ROWS) * GROUP + i0 // ROWS).astype(BF16)
    mine = mm(order, q_raw[...]).astype(BF16).reshape(NZ, 16, HEAD)
    q_send[...] = mine
    q_all[:, z] = mine
    eye = (i0 == i1).astype(BF16)

    pl.semaphore_wait(barrier, len(peers))

    q_copies = [
        send(q_send, q_all.at[:, z], sem_q, d - 1, dev(dz=d)) for d in range(1, NZ)
    ]
    t_copies, kv_copies = [], {}
    for r, (dy, dx) in enumerate(YX):
        if r == 0:
            continue
        back = YX.index(((NY - dy) % NY, dx))
        t_copies.append(
            send(turn.at[z, yx], turn.at[z, yx], sem_t, r, dev(dy=dy, dx=dx))
        )
        kv_copies[r] = (
            send(ck_in, k_all.at[back], sem_kv, 2 * back, dev(dy=dy, dx=dx)),
            send(cv_in, v_all.at[back], sem_kv, 2 * back + 1, dev(dy=dy, dx=dx)),
        )

    def arrived(sems, i, ref):
        pltpu.make_async_copy(ref, ref, sems.at[1, i]).wait()

    tokens = NYX * ROWS
    t0, t1 = iota((tokens, 128), 0), iota((tokens, 128), 1)
    docs = doc_ref[...]
    doc_wide = jnp.concatenate(
        [jnp.broadcast_to(docs[i : i + 1], (16, 128)) for i in range(NY)], axis=0
    )
    key_doc = jnp.sum(
        jnp.where(t1 == 16 * z + t0 % 16, doc_wide, 0), axis=1, keepdims=True
    )
    key_pos = 128 * (t0 // 16) + 16 * z + t0 % 16
    doc_mine = jnp.sum(jnp.where(iota((NY, 128), 0) == y, docs, 0), axis=0, keepdims=True)
    seen = i0 == 16 * (i1 // 16) + 8 * x + i1 % 8
    query_doc = mm(
        jnp.broadcast_to(doc_mine, (16, 128)).astype(BF16), seen.astype(BF16)
    )[:1].astype(jnp.int32)
    query_pos = 128 * y + 16 * (t1 // 16) + 8 * x + t1 % 8
    see = (key_pos <= query_pos) & (key_doc == query_doc)
    see = jnp.where(see, 0.0, NEG)
    see = jnp.concatenate([see, see], axis=1)

    pick_k = (t1 == (t0 // ROWS) * 16 + t0 % ROWS).astype(BF16)
    pick_v = (t1 == (t0 // ROWS) * 16 + ROWS + t0 % ROWS).astype(BF16)

    for i, cp in enumerate(q_copies):
        cp.wait()

    for g, pair in enumerate(PAIRS):
        for j in range(2):
            r = 2 * g + j
            if r == 0:
                get_k.wait()
                get_v.wait()
            else:
                arrived(sem_kv, 2 * r, k_all.at[r])
                arrived(sem_kv, 2 * r + 1, v_all.at[r])
        vt_all[g, :HEAD] = nt(eye, v_all[2 * g : 2 * g + 2].reshape(2 * KEYS, HEAD)).astype(BF16)
        vt_all[g, HEAD:] = jnp.ones((16, 2 * KEYS), BF16)
        biases = []
        for dy, dx in pair:
            source = ((y + dy) % NY * NZ + z) * NX + (x + dx) % NX
            for b in range(2):
                biases.append(jnp.where(mask_ref[y, 2 * source + b] == 1, 0.0, NEG))
        last = g == len(PAIRS) - 1
        if last:
            for r in range(1, NYX):
                t_copies[r - 1].wait()
            fresh = turn[z].reshape(128, HEAD)
            turn_k = mm(pick_k, fresh).astype(BF16)
            turn_v = nt(eye, mm(pick_v, fresh).astype(BF16)).astype(BF16)
            turn_v = jnp.concatenate([turn_v, jnp.ones((16, tokens), BF16)], axis=0)
            tt_copies = [
                send(turn.at[z], turn.at[z], sem_tt, d - 1, dev(dz=d)) for d in range(1, NZ)
            ]

        def block(i, carry, g=g, biases=biases, last=last):
            q = q_all[pl.ds(2 * i, 2)].reshape(256, HEAD)
            s = nt(k_all[2 * g : 2 * g + 2].reshape(2 * KEYS, HEAD), q)
            parts = [s[128 * b : 128 * (b + 1)] for b in range(4)]
            tops = [
                jnp.max(p, axis=0, keepdims=True) * SCALE + bias for p, bias in zip(parts, biases)
            ]
            if last:
                ts = nt(turn_k, q) * SCALE + see
                tops.append(jnp.max(ts, axis=0, keepdims=True))
            top = tops[0]
            for t in tops[1:]:
                top = jnp.maximum(top, t)
            if g == 0:
                top = jnp.maximum(top, FLOOR)
            else:
                old = peak[i, :1]
                top = jnp.maximum(top, old)
            p = jnp.concatenate(
                [
                    jnp.exp2(p * SCALE - (top - bias)).astype(BF16)
                    for p, bias in zip(parts, biases)
                ],
                axis=0,
            )
            o = mm(vt_all[g], p)
            if last:
                o = o + mm(turn_v, jnp.exp2(ts - top).astype(BF16))
            if g > 0:
                o = o + acc[i] * jnp.exp2(old - top)
            if last:
                for j in range(2):
                    at = 2 * i + j
                    lanes = slice(128 * j, 128 * (j + 1))
                    o_send[at] = o[:HEAD, lanes].astype(BF16)
                    st_send[at] = jnp.concatenate(
                        [top[:, lanes], o[HEAD : HEAD + 7, lanes]], axis=0
                    )
            else:
                acc[i] = o
                peak[i] = jnp.broadcast_to(top, (8, 256))
            return carry

        lax.fori_loop(0, 4, block, 0)

    rs_copies = []
    for d in range(1, NZ):
        to = (z + d) % NZ
        rs_copies.append(send(st_send.at[to], st_recv.at[z], sem_rs, 2 * d - 2, dev(dz=d)))
        rs_copies.append(send(o_send.at[to], o_recv.at[z], sem_rs, 2 * d - 1, dev(dz=d)))
    o_recv[z] = o_send[z]
    st_recv[z] = st_send[z]
    for cp in rs_copies:
        cp.wait()
    stats = [st_recv[j] for j in range(NZ)]
    top = stats[0][:1]
    for st in stats[1:]:
        top = jnp.maximum(top, st[:1])
    den, num = 0.0, 0.0
    for j, st in enumerate(stats):
        factor = jnp.exp2(st[:1] - top)
        den = den + factor * st[1:2]
        num = num + factor * o_recv[j].astype(F32)
    att = (num * (1.0 / den)).T.reshape(NZ, 2, ROWS, HEAD)
    att = jnp.concatenate(
        [att[:, 0].reshape(64, HEAD), att[:, 1].reshape(64, HEAD)], axis=1
    ).astype(BF16)
    part_a[z, yx] = att[:32]
    part_b[z, yx] = att[32:]

    a1 = [
        send(part_a.at[z, yx], part_a.at[z, yx], sem_a1, r, dev(dy=dy, dx=dx))
        for r, (dy, dx) in enumerate(YX)
        if r
    ]
    b1 = [
        send(part_b.at[z, yx], part_b.at[z, yx], sem_b1, d, dev(dz=d)) for d in range(1, NZ)
    ]
    get_w.wait()

    def project(part, z_of, row):
        terms[row] += mm(
            part[z_of].reshape(256, 256), w_all[pl.ds(pl.multiple_of(z_of * 256, 256), 256)]
        )

    terms[...] = jnp.zeros_like(terms)
    for cp in a1:
        cp.wait()

    def hop(step, way):
        at = (z - step * way) % NZ
        if step < 3:
            ref = part_a.at[at]
        else:
            ref = part_a.at[at, pl.ds(0, 4) if way == 1 else pl.ds(4, 4)]
        return send(ref, ref, sem_a2, 2 * step + (way + 1) // 2, dev(dz=way))

    right, left = hop(0, 1), hop(0, -1)
    for cp in b1:
        cp.wait()
    b2 = [
        send(part_b.at[:, yx], part_b.at[:, yx], sem_b2, r, dev(dy=dy, dx=dx))
        for r, (dy, dx) in enumerate(YX)
        if r
    ]
    project(part_a, z, 0)
    for step in range(1, 4):
        right.wait()
        left.wait()
        right, left = hop(step, 1), hop(step, -1)
        project(part_a, (z - step) % NZ, 0)
        project(part_a, (z + step) % NZ, 0)

    for cp in tt_copies:
        cp.wait()
    col = iota((128, 1024), 1)
    piece = 32 * (col // 32 % 4) + 4 * (col // 128) + 2 * (col // 16 % 2) + col // 4 % 2
    spread = (iota((128, 1024), 0) == piece).astype(BF16)
    slot_of = mm(
        jnp.broadcast_to(slot_ref[...], (16, 128)).astype(BF16), spread
    ).astype(jnp.int32)
    row, col = iota((16, 1024), 0), iota((16, 1024), 1)
    chosen = (slot_of == 4 * c + row // 4) & (col % 4 == row % 4)
    every = turn[...].reshape(1024, HEAD)
    kind = col // 8 % 2
    ak_ref[...] = mm((chosen & (kind == 0)).astype(BF16), every).astype(BF16)
    av_ref[...] = mm((chosen & (kind == 1)).astype(BF16), every).astype(BF16)

    right.wait()
    left.wait()
    project(part_a, (z + 4) % NZ, 0)
    for cp in b2:
        cp.wait()
    for j in range(NZ):
        project(part_b, j, 1)

    blocks = [terms.at[:, pl.ds(pl.multiple_of((2 * a + 1 - core) * 64, 64), 64)] for a in range(2)]
    for a in range(2):
        h_send[a] = blocks[a][...].astype(BF16)
    to_core = send(h_send, h_recv, sem_h, 0, dev(dcore=1))
    to_core.wait()

    def kept(a):
        rows = terms.at[:, pl.ds(pl.multiple_of((2 * a + core) * 64, 64), 64)]
        return rows[...] + h_recv[a].astype(F32)

    h_send[0] = kept(1 - xh).astype(BF16)
    to_chip = send(h_send.at[0], x_recv, sem_h, 1, dev(dxh=1))
    own = kept(xh)
    to_chip.wait()
    total = own + x_recv[...].astype(F32)
    for half in range(2):
        for low in range(4):
            for tx in range(NX):
                out_ref[pl.ds(16 * (4 * half + low) + 8 * tx, 8)] = total[
                    half, 32 * tx + 8 * low : 32 * tx + 8 * low + 8
                ]
    for sent in kv_copies.values():
        for cp in sent:
            cp.wait_send()


def on_device(
    queries, cache_keys, stored_cache_values, turn_keys, turn_values,
    block_mask, doc_ids, slot_ids, out_weight,
):
    anywhere = pl.BlockSpec(memory_space=pl.ANY)
    vmem = pl.BlockSpec(memory_space=pltpu.VMEM)
    smem = pl.BlockSpec(memory_space=pltpu.SMEM)
    sems = lambda n: pltpu.SemaphoreType.DMA((2, n))
    layer_out, append_keys, append_values = pl.pallas_call(
        kernel,
        out_shape=(
            jax.ShapeDtypeStruct((128, 256), F32),
            jax.ShapeDtypeStruct((16, HEAD), BF16),
            jax.ShapeDtypeStruct((16, HEAD), BF16),
        ),
        in_specs=[anywhere] * 4 + [vmem] * 4 + [smem],
        out_specs=(vmem, vmem, vmem),
        scratch_shapes=[
            pltpu.VMEM((128, HEAD), BF16),
            pltpu.VMEM((NZ, 16, HEAD), BF16),
            pltpu.VMEM((NZ, NZ, 16, HEAD), BF16),
            pltpu.VMEM((NYX, KEYS, HEAD), BF16),
            pltpu.VMEM((NYX, KEYS, HEAD), BF16),
            pltpu.VMEM((4, HEAD + 16, 2 * KEYS), BF16),
            pltpu.VMEM((2048, 256), BF16),
            pltpu.VMEM((NZ, NYX, 16, HEAD), BF16),
            pltpu.VMEM((4, 8, 256), F32),
            pltpu.VMEM((4, HEAD + 16, 256), F32),
            pltpu.VMEM((NZ, HEAD, 128), BF16),
            pltpu.VMEM((NZ, 8, 128), F32),
            pltpu.VMEM((NZ, HEAD, 128), BF16),
            pltpu.VMEM((NZ, 8, 128), F32),
            pltpu.VMEM((NZ, NYX, 32, 256), BF16),
            pltpu.VMEM((NZ, NYX, 32, 256), BF16),
            pltpu.VMEM((2, 256, 256), F32),
            pltpu.VMEM((2, 2, 64, 256), BF16),
            pltpu.VMEM((2, 2, 64, 256), BF16),
            pltpu.VMEM((2, 64, 256), BF16),
            pltpu.SemaphoreType.DMA((4,)),
            sems(7), sems(16), sems(8), sems(7), sems(14), sems(8), sems(8), sems(8), sems(8), sems(2),
        ],
        compiler_params=pltpu.CompilerParams(
            collective_id=0, has_side_effects=True, vmem_limit_bytes=32 * 1024 * 1024
        ),
        name="turn_attention",
    )(
        queries.reshape(128, HEAD),
        cache_keys.reshape(KEYS, HEAD),
        stored_cache_values.reshape(KEYS, HEAD),
        out_weight,
        turn_keys.reshape(ROWS, HEAD),
        turn_values.reshape(ROWS, HEAD),
        doc_ids.reshape(NY, 128),
        slot_ids.reshape(1, 128),
        block_mask,
    )
    return (
        layer_out,
        append_keys.reshape(16, 1, HEAD),
        append_values.reshape(16, 1, HEAD),
    )


def solution(mesh):
    placed = (
        P("ctx", "head", None),
        P("ctx", "head", None),
        P("ctx", "head", None),
        P("ctx", "head", None),
        P("ctx", "head", None),
        P(),
        P(),
        P(),
        P("head", "ctx"),
    )
    return jax.shard_map(
        on_device,
        mesh=mesh,
        in_specs=placed,
        out_specs=(P("head", "ctx"), P("ctx", "head", None), P("ctx", "head", None)),
        check_vma=False,
    )
```

time: 775 us -> 80.4 us (0.10)
  waiting for transfers between devices: 440 us -> 0 us
  blocking collectives: 259 us -> 0 us
  Pallas kernels: 0 us -> 73.2 us
  starting transfers between devices: 20.2 us -> 0 us
  matrix products: 14.4 us -> 0 us
  between operations: 14 us -> 0.69 us
  other arithmetic: 10.3 us -> 0 us
  local copies, waits for them, and re-layouts: 15.9 us -> 6.19 us
    all_gather x2 -> x0, waiting for transfers between devices: 309 us -> none  [the longest x1 309 us: on_device(): lax.all_gather(attended, 'ctx', axis=0, tiled=True)]
    all_gather x2 -> x0, blocking collectives: 259 us -> none  [the longest x1 135 us: on_device(): lax.all_gather(turn_keys, 'ctx', axis=0, tiled=True)]
    reduce_scatter x1 -> x0, waiting for transfers between devices: 74.8 us -> none  [on_device(): layer_out = lax.psum_scatter(terms, 'head', scatter_dimension=0, tiled=True)]
    pallas_call x0 -> x1, Pallas kernels: none -> 73.2 us  [on_device(): pl.pallas_call(kernel, out_shape=(jax.ShapeDtypeStruct((128, 256), F32),...]
    all_to_all x3 -> x0, waiting for transfers between devices: 56.9 us -> none  [the longest x1 49.3 us: on_device(): lax.all_to_all(out_flat, 'ctx', split_axis=0, concat_axis=0, tiled=True)]
    all_to_all x3 -> x0, starting transfers between devices: 20.1 us -> none  [the longest x1 10.9 us: on_device(): lax.all_to_all(out_flat, 'ctx', split_axis=0, concat_axis=0, tiled=True)]
    dot_general x5 -> x0, matrix products: 14.4 us -> none  [the longest x1 7.89 us: attend(): jnp.einsum('nkgm,mkd->nkgd', weights, value_rows, preferred_element_type=...]
  transfers between devices with their start and end apart: 6 -> 0, of which waited for: 4 -> 0; matrix products, arithmetic and copies ran while one was open for 3% -> 0% of each run, Pallas kernels for 0% -> 0%
where the time goes in v1:
time: 80.4 us; the launch traced here: 80.1 us
  Pallas kernels  73.2 us (91%)
  local copies, waits for them, and re-layouts  6.19 us (8%)
    pallas_call x1, Pallas kernels, on_device(): pl.pallas_call(kernel, out_shape=(jax.ShapeDtypeStruct((128, 256), F32),...  73.2 us
    unnamed x21, local copies, waits for them, and re-layouts  6.19 us

profile of v1, /device:TPU:1, one launch (start us, length us, event | category | flops | bytes accessed | tf_op | source)
XLA Modules:
  0.0 80.1 jit_solution(13817374481116732666)
XLA Ops:
  0.6 0.0 copy-start.7
  0.6 0.0 copy-start.6
  0.7 0.0 copy-start.5
  0.7 0.0 copy-start.4
  0.7 0.0 copy-start.8
  0.7 0.6 copy-done.7
  1.3 0.0 copy-done.6
  1.3 0.0 copy-done.5
  1.3 0.0 copy-done.4
  1.4 0.0 copy-done.8
  1.4 0.0 copy-start
  1.4 1.2 %copy-done = bf16[2048,256]{1,0:T(8,128)(2,1)S(1)} copy-done((bf16[2048,256]{1,0:T(8,128)(2,1)S(1)}, bf16[2048,256]{1,0:T(8,128)(2,1)}, u32[]{:S(2)}) %copy-start) | copy-done | bytes 1048600
  2.6 0.0 copy-start.1
  2.6 0.8 %copy-done.1 = bf16[256,1,128]{2,0,1:T(8,128)(2,1)S(1)} copy-done((bf16[256,1,128]{2,0,1:T(8,128)(2,1)S(1)}, bf16[256,1,128]{2,0,1:T(8,128)(2,1)}, u32[]{:S(2)}) %copy-start.1) | copy-done | bytes 65560
  3.4 0.0 copy-start.2
  3.4 0.8 %copy-done.2 = bf16[256,1,128]{2,0,1:T(8,128)(2,1)S(1)} copy-done((bf16[256,1,128]{2,0,1:T(8,128)(2,1)S(1)}, bf16[256,1,128]{2,0,1:T(8,128)(2,1)}, u32[]{:S(2)}) %copy-start.2) | copy-done | bytes 65560
  4.3 0.0 copy-start.3
  4.3 0.8 copy-done.3
  5.0 73.2 %turn_attention.1 = (f32[128,256]{1,0:T(8,128)S(1)}, bf16[16,128]{1,0:T(8,128)(2,1)S(1)}, bf16[16,128]{1,0:T(8,128)(2,1)S(1)}) custom-call(bf16[128,128]{1,0:T(8,128)(2,1)S(1)} %bitcast.11, bf16[256,128]{1,0:T(8,128)(2,1)S(1)} %bitcast.9, bf16[256,128]{1,0:T(8,128)(2,1)S(1)} %bitcast.10, bf16[2048,256]{1,0:T(8,128)(2,1)S(1)} %copy-done, ...), custom_call_target="tpu_custom_call" | custom-call | tf_op jit(solution)/shard_map/turn_attention/pallas_call | solution.py:338
  78.2 0.7 copy.15
  78.9 0.6 copy.16
  79.5 0.6 copy.17
Async XLA Ops:
  0.6 0.7 copy-start.7
  0.6 0.7 copy-start.6
  0.7 0.7 copy-start.5
  0.7 0.7 copy-start.4
  0.7 0.7 copy-start.8
  1.4 1.2 %copy-start = (bf16[2048,256]{1,0:T(8,128)(2,1)S(1)}, bf16[2048,256]{1,0:T(8,128)(2,1)}, u32[]{:S(2)}) copy-start(bf16[2048,256]{1,0:T(8,128)(2,1)} %w_in.1) | copy-start | bytes 3145732
  2.6 0.8 %copy-start.1 = (bf16[256,1,128]{2,0,1:T(8,128)(2,1)S(1)}, bf16[256,1,128]{2,0,1:T(8,128)(2,1)}, u32[]{:S(2)}) copy-start(bf16[256,1,128]{2,0,1:T(8,128)(2,1)} %param.10) | copy-start | bytes 196612
  3.4 0.8 %copy-start.2 = (bf16[256,1,128]{2,0,1:T(8,128)(2,1)S(1)}, bf16[256,1,128]{2,0,1:T(8,128)(2,1)}, u32[]{:S(2)}) copy-start(bf16[256,1,128]{2,0,1:T(8,128)(2,1)} %param.11) | copy-start | bytes 196612
  4.3 0.8 copy-start.3

commit v2 on v1

v2 whole, which is shorter than its diff:
```python
import math

import jax
import jax.numpy as jnp
from jax import lax
from jax.experimental import pallas as pl
from jax.experimental.pallas import tpu as pltpu
from jax.sharding import PartitionSpec as P

MESH = pl.DeviceIdType.MESH
F32 = jnp.float32
BF16 = jnp.bfloat16

NY, NZ, NX = 4, 8, 2
NYX = NY * NX
NH = 4
HEAD = 128
KEYS = 256
GROUP = 16
ROWS = 8
NEG = -1e30
FLOOR = -1e29
SCALE = math.log2(math.e) / math.sqrt(HEAD)

YX = [(0, 0), (0, 1), (1, 0), (1, 1), (3, 0), (3, 1), (2, 0), (2, 1)]
YX_ORDER = [1, 2, 4, 3, 5, 6, 7]
ZS = [0, 1, 7, 2, 6, 3, 5, 4]
Z_ORDER = [1, 7, 2, 6, 3, 5, 4]
Z_BATCHES = [(0, 1), (1, 3), (3, 5), (5, 8)]


def nt(a, b):
    return lax.dot_general(a, b, (((1,), (1,)), ((), ())), preferred_element_type=F32)


def mm(a, b):
    return jnp.dot(a, b, preferred_element_type=F32)


def iota(shape, dim):
    return lax.broadcasted_iota(jnp.int32, shape, dim)


def back_yx(r):
    dy, dx = YX[r]
    return YX.index(((NY - dy) % NY, dx))


def kernel(
    q_in, ck_in, cv_in, w_in, tk_in, tv_in, doc_in, slot_in, mask_in,
    out_ref, ak_ref, av_ref,
    q_raw, q_send, q_all, k_all, v_all, v_wide, w_all, turn, tk, tv, docs_ref, slots_ref, mask_ref,
    peak, acc, o_send, st_send, o_recv, st_recv, part_a, part_b, sum_a, sum_b,
    ha_send, ha_recv, hb_send, hb_recv,
    sem_in, sem_q, sem_kv, sem_t, sem_tt, sem_rs, sem_a1, sem_b1, sem_a2, sem_b2, sem_h,
):
    c = lax.axis_index("ctx")
    h = lax.axis_index("head")
    y, z, x = c // (NZ * NX), (c // NX) % NZ, c % NX
    yx = y * NX + x

    def dev(dy=0, dz=0, dx=0, dh=0):
        ty, tz, tx = (y + dy) % NY, (z + dz) % NZ, (x + dx) % NX
        return ((ty * NZ + tz) * NX + tx, (h + dh) % NH)

    def to_yx(r):
        return dev(dy=YX[r][0], dx=YX[r][1])

    def send(src, dst, sems, i, device):
        copy = pltpu.make_async_remote_copy(
            src_ref=src, dst_ref=dst, send_sem=sems.at[0, i], recv_sem=sems.at[1, i],
            device_id=device, device_id_type=MESH,
        )
        copy.start()
        return copy

    def arrived(ref, sems, i):
        pltpu.make_async_copy(ref, ref, sems.at[1, i]).wait()

    def fetch(src, dst, i):
        copy = pltpu.make_async_copy(src, dst, sem_in.at[i])
        copy.start()
        return copy

    get_q = fetch(q_in, q_raw, 0)
    get_small = [
        fetch(tk_in, tk, 1), fetch(tv_in, tv, 2), fetch(doc_in, docs_ref, 3),
        fetch(slot_in, slots_ref, 4), fetch(mask_in, mask_ref, 5),
    ]
    get_kv = [fetch(ck_in, k_all.at[0], 6), fetch(cv_in, v_all.at[0], 7)]
    get_w = fetch(w_in, w_all, 8)

    barrier = pltpu.get_barrier_semaphore()
    peers = [to_yx(r) for r in YX_ORDER] + [dev(dz=d) for d in Z_ORDER]
    peers += [dev(dh=d) for d in range(1, NH)]
    for p in peers:
        pl.semaphore_signal(barrier, inc=1, device_id=p, device_id_type=MESH)

    get_q.wait()
    i0, i1 = iota((128, 128), 0), iota((128, 128), 1)
    order = (i1 == (i0 % ROWS) * GROUP + i0 // ROWS).astype(BF16)
    mine = mm(order, q_raw[...]).astype(BF16).reshape(NZ, 16, HEAD)
    q_send[...] = mine
    q_all[:, z] = mine
    for cp in get_small:
        cp.wait()
    turn[z, yx] = jnp.concatenate([tk[...].astype(F32), tv[...].astype(F32)], axis=0).astype(BF16)

    pl.semaphore_wait(barrier, len(peers))

    q_copies = [send(q_send, q_all.at[:, z], sem_q, d, dev(dz=d)) for d in Z_ORDER]
    kv_copies, t_copies = [], []
    for r in YX_ORDER:
        b = back_yx(r)
        kv_copies.append(send(ck_in, k_all.at[b], sem_kv, 2 * b, to_yx(r)))
        kv_copies.append(send(cv_in, v_all.at[b], sem_kv, 2 * b + 1, to_yx(r)))
        t_copies.append(send(turn.at[z, yx], turn.at[z, yx], sem_t, r, to_yx(r)))

    docs = docs_ref[...]
    key_token = 16 * z + 8 * (i1 // 16 % 2) + i1 % 8
    by_y = mm(
        jnp.concatenate([docs.astype(F32), jnp.zeros((12, 128), F32)], axis=0).astype(BF16),
        (i0 == key_token).astype(BF16),
    )
    key_doc = jnp.sum(
        jnp.where(iota((16, 128), 0) == iota((16, 128), 1) // 32, by_y, 0.0), axis=0, keepdims=True
    )
    doc_mine = jnp.sum(
        jnp.where(iota((NY, 128), 0) == y, docs, 0), axis=0, keepdims=True
    ).astype(F32)
    query_token = 16 * (i0 // 16) + 8 * x + i0 % 8
    query_doc = jnp.sum(jnp.where(i1 == query_token, doc_mine, 0.0), axis=1, keepdims=True)
    see = (
        (128 * (i1 // 32) + key_token <= 128 * y + query_token)
        & (key_doc == query_doc)
        & (i1 // 8 % 2 == 0)
    )
    see = jnp.where(see, 0.0, NEG)
    see = jnp.concatenate([see, see], axis=0)
    diagonal = i0 == i1

    for cp in q_copies:
        cp.wait()

    for g in range(4):
        for r in (2 * g, 2 * g + 1):
            if r == 0:
                for cp in get_kv:
                    cp.wait()
            else:
                arrived(k_all.at[r], sem_kv, 2 * r)
                arrived(v_all.at[r], sem_kv, 2 * r + 1)
        v_wide[:, :HEAD] = v_all[2 * g : 2 * g + 2].reshape(2 * KEYS, HEAD)
        v_wide[:, HEAD:] = jnp.ones((2 * KEYS, HEAD), BF16)
        biases = []
        for dy, dx in YX[2 * g : 2 * g + 2]:
            source = ((y + dy) % NY * NZ + z) * NX + (x + dx) % NX
            for b in range(2):
                biases.append(jnp.where(mask_ref[y, 2 * source + b] == 1, 0.0, NEG))
        last = g == 3
        if last:
            for cp in t_copies:
                cp.wait()
            fresh = turn[z].reshape(128, HEAD)
            fresh_v = mm((i1 == i0 + 8).astype(BF16), fresh).astype(BF16)
            fresh_v = jnp.concatenate([fresh_v, jnp.ones((128, HEAD), BF16)], axis=1)
            tt_copies = [send(turn.at[z], turn.at[z], sem_tt, d, dev(dz=d)) for d in Z_ORDER]
        for i in range(4):
            q = q_all[2 * i : 2 * i + 2].reshape(256, HEAD)
            s = nt(q, k_all[2 * g : 2 * g + 2].reshape(2 * KEYS, HEAD))
            parts = [s[:, 128 * b : 128 * (b + 1)] * SCALE + biases[b] for b in range(4)]
            values = v_wide[...]
            if last:
                parts.append(nt(q, fresh) * SCALE + see)
                values = jnp.concatenate([values, fresh_v], axis=0)
            top = parts[0]
            for p in parts[1:]:
                top = jnp.maximum(top, p)
            top = jnp.broadcast_to(jnp.max(top, axis=1, keepdims=True), (256, 128))
            old = FLOOR if g == 0 else peak[i]
            top = jnp.maximum(top, old)
            p = jnp.concatenate([jnp.exp2(p - top).astype(BF16) for p in parts], axis=1)
            o = mm(p, values)
            if g > 0:
                keep = jnp.exp2(old - top)
                o = o + acc[i] * jnp.concatenate([keep, keep], axis=1)
            if not last:
                acc[i] = o
                peak[i] = top
                continue
            for j in range(2):
                rows = slice(128 * j, 128 * (j + 1))
                o_send[2 * i + j] = o[rows, :HEAD].astype(BF16)
                st_send[2 * i + j] = jnp.concatenate(
                    [
                        jnp.sum(jnp.where(diagonal, top[rows], 0.0), axis=0, keepdims=True),
                        jnp.sum(jnp.where(diagonal, o[rows, HEAD:], 0.0), axis=0, keepdims=True),
                        jnp.zeros((6, 128), F32),
                    ],
                    axis=0,
                )

    halves = (pl.ds(0, 64), pl.ds(64, 64))
    rs = [[], []]
    for d in Z_ORDER:
        to = (z + d) % NZ
        rs[0].append(send(st_send.at[to], st_recv.at[z], sem_rs, d, dev(dz=d)))
    for half in range(2):
        for d in Z_ORDER:
            to = (z + d) % NZ
            rs[half].append(
                send(
                    o_send.at[to, halves[half]], o_recv.at[z, halves[half]],
                    sem_rs, 8 * (half + 1) + d, dev(dz=d),
                )
            )
    o_recv[z] = o_send[z]
    st_recv[z] = st_send[z]
    for cp in rs[0]:
        cp.wait()
    peaks = jnp.concatenate([st_recv[j, 0:1] for j in range(NZ)], axis=0)
    totals = jnp.concatenate([st_recv[j, 1:2] for j in range(NZ)], axis=0)
    factor = jnp.exp2(peaks - jnp.max(peaks, axis=0, keepdims=True))
    factor = factor / jnp.sum(factor * totals, axis=0, keepdims=True)
    factor = jnp.concatenate([factor, jnp.zeros((120, 128), F32)], axis=0).T

    def attended(half):
        rows = slice(64 * half, 64 * (half + 1))
        num = 0.0
        for j in range(NZ):
            num = num + factor[rows, j : j + 1] * o_recv[j, halves[half]].astype(F32)
        num = num.reshape(4, 2, ROWS, HEAD)
        return jnp.concatenate(
            [num[:, 0].reshape(32, HEAD), num[:, 1].reshape(32, HEAD)], axis=1
        ).astype(BF16)

    part_a[0, 0] = attended(0)
    a1 = {r: send(part_a.at[0, 0], part_a.at[0, back_yx(r)], sem_a1, back_yx(r), to_yx(r)) for r in YX_ORDER}
    for cp in rs[1]:
        cp.wait()
    part_b[0, 0] = attended(1)
    b1 = [
        send(part_b.at[0, 0], part_b.at[ZS.index(NZ - d), 0], sem_b1, ZS.index(NZ - d), dev(dz=d))
        for d in Z_ORDER
    ]
    b2, a2 = [], []

    def spread(batch):
        lo, hi = Z_BATCHES[batch]
        for s in range(lo, hi):
            if s:
                arrived(part_b.at[s, 0], sem_b1, s)
        for r in YX_ORDER:
            b = back_yx(r)
            b2.append(
                send(
                    part_b.at[pl.ds(lo, hi - lo), 0], part_b.at[pl.ds(lo, hi - lo), b],
                    sem_b2, 8 * batch + b, to_yx(r),
                )
            )

    def spread_arrived(batch):
        lo, hi = Z_BATCHES[batch]
        for r in YX_ORDER:
            arrived(part_b.at[pl.ds(lo, hi - lo), r], sem_b2, 8 * batch + r)

    def piece(slot, p):
        return part_a.at[slot, pl.ds(2 * p, 2)]

    def index(hop, way, p):
        return 8 * hop + 4 * way + p

    def pass_on(hop, p, both=True):
        for way, (step, src, dst) in enumerate((
            (1, (NZ - hop) % NZ, NZ - 1 - hop), (-1, hop, hop + 1),
        )):
            if hop == 3:
                if p // 2 != way:
                    continue
                step, src, dst = 2 * step, (6, 2)[way], 4
            a2.append(send(piece(src, p), piece(dst, p), sem_a2, index(hop, way, p), dev(dz=step)))

    def passed(hop, p):
        for way in range(2):
            dst = (NZ - 1 - hop, hop + 1)[way]
            if hop == 3:
                if p // 2 != way:
                    continue
                dst = 4
            arrived(piece(dst, p), sem_a2, index(hop, way, p))

    def weight(dz):
        at = pl.multiple_of((z + dz) % NZ * 256, 256)
        return w_all[pl.ds(at, 256)]

    def project_a(slot):
        part = mm(part_a[slot].reshape(256, 256), weight(slot))
        sum_a[...] = part if slot == 0 else sum_a[...] + part

    def project_b(batch):
        lo, hi = Z_BATCHES[batch]
        part = 0.0
        for s in range(lo, hi):
            part = part + mm(part_b[s].reshape(256, 256), weight(ZS[s]))
        sum_b[...] = part if batch == 0 else sum_b[...] + part

    spread(0)
    for p in range(4):
        for r in (2 * p, 2 * p + 1):
            if r:
                arrived(part_a.at[0, r], sem_a1, r)
        pass_on(0, p)
        if p == 1:
            spread(1)
    spread(2)
    get_w.wait()
    project_a(0)
    for p in range(4):
        passed(0, p)
        pass_on(1, p)
        if p == 0:
            spread(3)
    spread_arrived(0)
    project_a(1)
    project_a(7)
    project_b(0)
    for p in range(4):
        passed(1, p)
        pass_on(2, p)
        pass_on(3, p)
    project_a(2)
    project_a(6)

    for cp in tt_copies:
        cp.wait()
    col = iota((128, 1024), 1)
    of_piece = 32 * (col // 32 % 4) + 4 * (col // 128) + 2 * (col // 16 % 2) + col // 4 % 2
    slot_of = mm(
        jnp.broadcast_to(slots_ref[...], (16, 128)).astype(BF16),
        (iota((128, 1024), 0) == of_piece).astype(BF16),
    ).astype(jnp.int32)
    row, col = iota((16, 1024), 0), iota((16, 1024), 1)
    chosen = (slot_of == 4 * c + row // 4) & (col % 4 == row % 4)
    every = turn[...].reshape(1024, HEAD)
    kind = col // 8 % 2
    ak_ref[...] = mm((chosen & (kind == 0)).astype(BF16), every).astype(BF16)
    av_ref[...] = mm((chosen & (kind == 1)).astype(BF16), every).astype(BF16)

    def rows_of(head):
        dy = (head + NY - y) % NY
        return pl.ds(pl.multiple_of(64 * jnp.where(dy >= 2, 5 - dy, dy), 64), 64)

    def share(total, sent, got, base):
        copies = []
        for d in (2, 3, 1):
            sent[d - 1] = total[rows_of((h + d) % NH)].astype(BF16)
            copies.append(send(sent.at[d - 1], got.at[3 - d], sem_h, base + 3 - d, dev(dh=d)))
        return copies

    def finish(total, got, copies, first):
        for cp in copies:
            cp.wait()
        whole = total[rows_of(h)]
        for j in range(3):
            whole = whole + got[j].astype(F32)
        for dx in range(NX):
            for j in range(4):
                at = 16 * (first + j) + 8 * ((x + dx) % NX)
                out_ref[pl.ds(pl.multiple_of(at, 8), 8)] = whole[
                    32 * dx + 8 * j : 32 * dx + 8 * j + 8
                ]

    for batch in range(1, 4):
        spread_arrived(batch)
        project_b(batch)
    to_b = share(sum_b, hb_send, hb_recv, 0)
    for p in range(4):
        passed(2, p)
    project_a(3)
    project_a(5)
    for p in range(4):
        passed(3, p)
    project_a(4)
    to_a = share(sum_a, ha_send, ha_recv, 3)
    finish(sum_b, hb_recv, to_b, 4)
    for cp in kv_copies + list(a1.values()) + b1 + b2 + a2:
        cp.wait_send()
    finish(sum_a, ha_recv, to_a, 0)


def on_device(
    queries, cache_keys, stored_cache_values, turn_keys, turn_values,
    block_mask, doc_ids, slot_ids, out_weight,
):
    anywhere = pl.BlockSpec(memory_space=pl.ANY)
    vmem = pl.BlockSpec(memory_space=pltpu.VMEM)
    sems = lambda n: pltpu.SemaphoreType.DMA((2, n))
    layer_out, append_keys, append_values = pl.pallas_call(
        kernel,
        out_shape=(
            jax.ShapeDtypeStruct((128, 256), F32),
            jax.ShapeDtypeStruct((16, HEAD), BF16),
            jax.ShapeDtypeStruct((16, HEAD), BF16),
        ),
        in_specs=[anywhere] * 9,
        out_specs=(vmem, vmem, vmem),
        scratch_shapes=[
            pltpu.VMEM((128, HEAD), BF16),
            pltpu.VMEM((NZ, 16, HEAD), BF16),
            pltpu.VMEM((NZ, NZ, 16, HEAD), BF16),
            pltpu.VMEM((NYX, KEYS, HEAD), BF16),
            pltpu.VMEM((NYX, KEYS, HEAD), BF16),
            pltpu.VMEM((2 * KEYS, 2 * HEAD), BF16),
            pltpu.VMEM((2048, 256), BF16),
            pltpu.VMEM((NZ, NYX, 16, HEAD), BF16),
            pltpu.VMEM((ROWS, HEAD), BF16),
            pltpu.VMEM((ROWS, HEAD), BF16),
            pltpu.VMEM((NY, 128), jnp.int32),
            pltpu.VMEM((1, 128), jnp.int32),
            pltpu.SMEM((NY, 128), jnp.int32),
            pltpu.VMEM((4, 256, 128), F32),
            pltpu.VMEM((4, 256, 256), F32),
            pltpu.VMEM((NZ, 128, HEAD), BF16),
            pltpu.VMEM((NZ, 8, 128), F32),
            pltpu.VMEM((NZ, 128, HEAD), BF16),
            pltpu.VMEM((NZ, 8, 128), F32),
            pltpu.VMEM((NZ, NYX, 32, 256), BF16),
            pltpu.VMEM((NZ, NYX, 32, 256), BF16),
            pltpu.VMEM((256, 256), F32),
            pltpu.VMEM((256, 256), F32),
            pltpu.VMEM((3, 64, 256), BF16),
            pltpu.VMEM((3, 64, 256), BF16),
            pltpu.VMEM((3, 64, 256), BF16),
            pltpu.VMEM((3, 64, 256), BF16),
            pltpu.SemaphoreType.DMA((9,)),
            sems(8), sems(16), sems(8), sems(8), sems(24), sems(8), sems(8), sems(32), sems(32), sems(6),
        ],
        compiler_params=pltpu.CompilerParams(
            collective_id=0, has_side_effects=True, vmem_limit_bytes=60 * 1024 * 1024
        ),
        name="turn_attention",
    )(
        queries.reshape(128, HEAD),
        cache_keys.reshape(KEYS, HEAD),
        stored_cache_values.reshape(KEYS, HEAD),
        out_weight,
        turn_keys.reshape(ROWS, HEAD),
        turn_values.reshape(ROWS, HEAD),
        doc_ids.reshape(NY, 128),
        slot_ids.reshape(1, 128),
        block_mask,
    )
    return (
        layer_out,
        append_keys.reshape(16, 1, HEAD),
        append_values.reshape(16, 1, HEAD),
    )


def solution(mesh):
    placed = (
        P("ctx", "head", None),
        P("ctx", "head", None),
        P("ctx", "head", None),
        P("ctx", "head", None),
        P("ctx", "head", None),
        P(),
        P(),
        P(),
        P("head", "ctx"),
    )
    return jax.shard_map(
        on_device,
        mesh=mesh,
        in_specs=placed,
        out_specs=(P("head", "ctx"), P("ctx", "head", None), P("ctx", "head", None)),
        check_vma=False,
    )
```

time: 80.4 us -> 67.7 us (0.84)
  Pallas kernels: 73.2 us -> 64.1 us
  local copies, waits for them, and re-layouts: 6.19 us -> 2.84 us
    pallas_call x1, Pallas kernels: 73.2 us -> 64.1 us  [on_device(): pl.pallas_call(kernel, out_shape=(jax.ShapeDtypeStruct((128, 256), F32),...]
    unnamed x21 -> x7, local copies, waits for them, and re-layouts: 6.19 us -> 2.84 us
where the time goes in v2:
time: 67.7 us; the launch traced here: 67.6 us
  Pallas kernels  64.1 us (95%)
  local copies, waits for them, and re-layouts  2.84 us (4%)
    pallas_call x1, Pallas kernels, on_device(): pl.pallas_call(kernel, out_shape=(jax.ShapeDtypeStruct((128, 256), F32),...  64.1 us
    unnamed x7, local copies, waits for them, and re-layouts  2.84 us

profile of v2, /device:TPU:1, one launch (start us, length us, event | category | flops | bytes accessed | tf_op | source)
XLA Modules:
  0.0 67.6 jit_solution(12398390678466025261)
XLA Ops:
  0.6 64.1 %turn_attention.1 = (f32[128,256]{1,0:T(8,128)}, bf16[16,128]{1,0:T(8,128)(2,1)}, bf16[16,128]{1,0:T(8,128)(2,1)}) custom-call(bf16[128,128]{1,0:T(8,128)(2,1)} %bitcast.11, bf16[256,128]{1,0:T(8,128)(2,1)} %bitcast.9, bf16[256,128]{1,0:T(8,128)(2,1)} %bitcast.10, bf16[2048,256]{1,0:T(8,128)(2,1)} %w_in.1, bf16[8,128]{1,0:T(8,128)(2,1)} %bitcast.14, ...), custom_call_target="tpu_custom_call" | custom-call | tf_op jit(solution)/shard_map/turn_attention/pallas_call | solution.py:398
  64.7 0.0 copy-start.1
  64.7 1.6 %copy.15 = f32[128,256]{1,0:T(8,128)} copy(f32[128,256]{1,0:T(8,128)} %get-tuple-element.12) | data formatting | bytes 262144
  66.3 0.0 copy-done.1
  66.3 0.0 copy-start
  66.3 0.6 copy.16
  66.9 0.1 copy-done
  67.0 0.6 copy.17
Async XLA Ops:
  64.7 1.6 %copy-start.1 = (bf16[16,128]{1,0:T(8,128)(2,1)S(1)}, bf16[16,128]{1,0:T(8,128)(2,1)}, u32[]{:S(2)}) copy-start(bf16[16,128]{1,0:T(8,128)(2,1)} %get-tuple-element.7) | copy-start | bytes 12292
  66.3 0.7 copy-start

commit v3 on v2

--- a/solution.py
+++ b/solution.py
@@ -27,6 +27,11 @@
 ZS = [0, 1, 7, 2, 6, 3, 5, 4]
 Z_ORDER = [1, 7, 2, 6, 3, 5, 4]
 Z_BATCHES = [(0, 1), (1, 3), (3, 5), (5, 8)]
+KEY_GROUPS = [(0, 1), (2, 4), (6, 3), (5, 7)]
+BLOCKS = [
+    (0, 0), (0, 1), (1, 0), (1, 1), (0, 2), (1, 2), (2, 0), (2, 1), (2, 2), (0, 3), (1, 3), (2, 3),
+    (3, 0), (3, 1), (3, 2), (3, 3),
+]
 
 
 def nt(a, b):
@@ -49,10 +54,10 @@
 def kernel(
     q_in, ck_in, cv_in, w_in, tk_in, tv_in, doc_in, slot_in, mask_in,
     out_ref, ak_ref, av_ref,
-    q_raw, q_send, q_all, k_all, v_all, v_wide, w_all, turn, tk, tv, docs_ref, slots_ref, mask_ref,
-    peak, acc, o_send, st_send, o_recv, st_recv, part_a, part_b, sum_a, sum_b,
+    q_raw, q_all, k_all, v_all, v_wide, w_all, turn_yx, turn_all, tk, tv, docs_ref, slots_ref, mask_ref,
+    peak, acc, o_send, st_send, o_recv, st_recv, factors, part_a, part_b, sum_a, sum_b,
     ha_send, ha_recv, hb_send, hb_recv,
-    sem_in, sem_q, sem_kv, sem_t, sem_tt, sem_rs, sem_a1, sem_b1, sem_a2, sem_b2, sem_h,
+    sem_in, sem_q, sem_kv, sem_t, sem_tz, sem_tt, sem_rs, sem_a1, sem_b1, sem_a2, sem_b2, sem_h,
 ):
     c = lax.axis_index("ctx")
     h = lax.axis_index("head")
@@ -99,22 +104,30 @@
     get_q.wait()
     i0, i1 = iota((128, 128), 0), iota((128, 128), 1)
     order = (i1 == (i0 % ROWS) * GROUP + i0 // ROWS).astype(BF16)
-    mine = mm(order, q_raw[...]).astype(BF16).reshape(NZ, 16, HEAD)
-    q_send[...] = mine
-    q_all[:, z] = mine
+    q_all[0] = mm(order, q_raw[...]).astype(BF16)
     for cp in get_small:
         cp.wait()
-    turn[z, yx] = jnp.concatenate([tk[...].astype(F32), tv[...].astype(F32)], axis=0).astype(BF16)
+    mine = jnp.concatenate([tk[...].astype(F32), tv[...].astype(F32)], axis=0).astype(BF16)
+    turn_yx[yx] = mine
+    turn_all[z, yx] = mine
 
     pl.semaphore_wait(barrier, len(peers))
 
-    q_copies = [send(q_send, q_all.at[:, z], sem_q, d, dev(dz=d)) for d in Z_ORDER]
-    kv_copies, t_copies = [], []
-    for r in YX_ORDER:
-        b = back_yx(r)
-        kv_copies.append(send(ck_in, k_all.at[b], sem_kv, 2 * b, to_yx(r)))
-        kv_copies.append(send(cv_in, v_all.at[b], sem_kv, 2 * b + 1, to_yx(r)))
-        t_copies.append(send(turn.at[z, yx], turn.at[z, yx], sem_t, r, to_yx(r)))
+    def give_k(src, slot, device):
+        return send(src, k_all.at[slot], sem_kv, 2 * slot, device)
+
+    def give_v(src, slot, device):
+        return send(src, v_all.at[slot], sem_kv, 2 * slot + 1, device)
+
+    q_copies = {d: send(q_all.at[0], q_all.at[ZS.index(NZ - d)], sem_q, ZS.index(NZ - d), dev(dz=d)) for d in Z_ORDER}
+    kv_copies = [give_v(cv_in, 1, to_yx(1))]
+    for r in (2, 4, 6):
+        kv_copies.append(give_k(ck_in, back_yx(r), to_yx(r)))
+    kv_copies.append(give_k(ck_in, 1, to_yx(1)))
+    for r in (2, 4, 6):
+        kv_copies.append(give_v(cv_in, back_yx(r), to_yx(r)))
+    t_copies = [send(turn_yx.at[yx], turn_yx.at[yx], sem_t, r, to_yx(r)) for r in YX_ORDER]
+    tz_copies = [send(turn_yx.at[yx], turn_all.at[z, yx], sem_tz, d, dev(dz=d)) for d in Z_ORDER]
 
     docs = docs_ref[...]
     key_token = 16 * z + 8 * (i1 // 16 % 2) + i1 % 8
@@ -128,111 +141,132 @@
     doc_mine = jnp.sum(
         jnp.where(iota((NY, 128), 0) == y, docs, 0), axis=0, keepdims=True
     ).astype(F32)
-    query_token = 16 * (i0 // 16) + 8 * x + i0 % 8
-    query_doc = jnp.sum(jnp.where(i1 == query_token, doc_mine, 0.0), axis=1, keepdims=True)
-    see = (
-        (128 * (i1 // 32) + key_token <= 128 * y + query_token)
-        & (key_doc == query_doc)
-        & (i1 // 8 % 2 == 0)
-    )
-    see = jnp.where(see, 0.0, NEG)
-    see = jnp.concatenate([see, see], axis=0)
+    right_key = (i1 // 8 % 2 == 0)
+
+    def sight(slot):
+        query_token = 16 * ((z + ZS[slot]) % NZ) + 8 * x + i0 % 8
+        query_doc = jnp.sum(jnp.where(i1 == query_token, doc_mine, 0.0), axis=1, keepdims=True)
+        see = (
+            (128 * (i1 // 32) + key_token <= 128 * y + query_token)
+            & (key_doc == query_doc)
+            & right_key
+        )
+        return jnp.where(see, 0.0, NEG)
+
     diagonal = i0 == i1
 
-    for cp in q_copies:
-        cp.wait()
-
-    for g in range(4):
-        for r in (2 * g, 2 * g + 1):
-            if r == 0:
-                for cp in get_kv:
+    arrived(v_all.at[1], sem_kv, 3)
+    for r in (2, 4, 6):
+        kv_copies.append(give_v(v_all.at[1], back_yx(r + 1), to_yx(r)))
+    for r in (2, 4, 6):
+        arrived(k_all.at[r], sem_kv, 2 * r)
+        kv_copies.append(give_k(k_all.at[r], r + 1, to_yx(1)))
+
+    have = {("k", 2), ("k", 4), ("k", 6), ("v", 1)}
+    biases = {}
+    for g, i in BLOCKS:
+        last = g == 3
+        if i == 0:
+            for j, r in enumerate(KEY_GROUPS[g]):
+                if r == 0:
+                    for cp in get_kv:
+                        cp.wait()
+                else:
+                    if ("k", r) not in have:
+                        arrived(k_all.at[r], sem_kv, 2 * r)
+                    if ("v", r) not in have:
+                        arrived(v_all.at[r], sem_kv, 2 * r + 1)
+                v_wide[g, KEYS * j : KEYS * (j + 1), :HEAD] = v_all[r]
+            v_wide[g, :, HEAD:] = jnp.ones((2 * KEYS, HEAD), BF16)
+            biases[g] = []
+            for r in KEY_GROUPS[g]:
+                source = ((y + YX[r][0]) % NY * NZ + z) * NX + (x + YX[r][1]) % NX
+                for b in range(2):
+                    biases[g].append(jnp.where(mask_ref[y, 2 * source + b] == 1, 0.0, NEG))
+            if last:
+                for cp in t_copies:
                     cp.wait()
-            else:
-                arrived(k_all.at[r], sem_kv, 2 * r)
-                arrived(v_all.at[r], sem_kv, 2 * r + 1)
-        v_wide[:, :HEAD] = v_all[2 * g : 2 * g + 2].reshape(2 * KEYS, HEAD)
-        v_wide[:, HEAD:] = jnp.ones((2 * KEYS, HEAD), BF16)
-        biases = []
-        for dy, dx in YX[2 * g : 2 * g + 2]:
-            source = ((y + dy) % NY * NZ + z) * NX + (x + dx) % NX
-            for b in range(2):
-                biases.append(jnp.where(mask_ref[y, 2 * source + b] == 1, 0.0, NEG))
-        last = g == 3
+                fresh = turn_yx[...].reshape(128, HEAD)
+                fresh_v = mm((i1 == i0 + 8).astype(BF16), fresh).astype(BF16)
+                fresh_v = jnp.concatenate([fresh_v, jnp.ones((128, HEAD), BF16)], axis=1)
+        if g == 0:
+            for slot in (2 * i, 2 * i + 1):
+                if slot:
+                    arrived(q_all.at[slot], sem_q, slot)
+        q = q_all[2 * i : 2 * i + 2].reshape(256, HEAD)
+        parts = []
+        for j, r in enumerate(KEY_GROUPS[g]):
+            s = nt(q, k_all[r])
+            parts += [
+                s[:, :128] * SCALE + biases[g][2 * j], s[:, 128:] * SCALE + biases[g][2 * j + 1]
+            ]
+        values = v_wide[g]
         if last:
-            for cp in t_copies:
-                cp.wait()
-            fresh = turn[z].reshape(128, HEAD)
-            fresh_v = mm((i1 == i0 + 8).astype(BF16), fresh).astype(BF16)
-            fresh_v = jnp.concatenate([fresh_v, jnp.ones((128, HEAD), BF16)], axis=1)
-            tt_copies = [send(turn.at[z], turn.at[z], sem_tt, d, dev(dz=d)) for d in Z_ORDER]
-        for i in range(4):
-            q = q_all[2 * i : 2 * i + 2].reshape(256, HEAD)
-            s = nt(q, k_all[2 * g : 2 * g + 2].reshape(2 * KEYS, HEAD))
-            parts = [s[:, 128 * b : 128 * (b + 1)] * SCALE + biases[b] for b in range(4)]
-            values = v_wide[...]
-            if last:
-                parts.append(nt(q, fresh) * SCALE + see)
-                values = jnp.concatenate([values, fresh_v], axis=0)
-            top = parts[0]
-            for p in parts[1:]:
-                top = jnp.maximum(top, p)
-            top = jnp.broadcast_to(jnp.max(top, axis=1, keepdims=True), (256, 128))
-            old = FLOOR if g == 0 else peak[i]
-            top = jnp.maximum(top, old)
-            p = jnp.concatenate([jnp.exp2(p - top).astype(BF16) for p in parts], axis=1)
-            o = mm(p, values)
-            if g > 0:
-                keep = jnp.exp2(old - top)
-                o = o + acc[i] * jnp.concatenate([keep, keep], axis=1)
-            if not last:
-                acc[i] = o
-                peak[i] = top
-                continue
-            for j in range(2):
-                rows = slice(128 * j, 128 * (j + 1))
-                o_send[2 * i + j] = o[rows, :HEAD].astype(BF16)
-                st_send[2 * i + j] = jnp.concatenate(
-                    [
-                        jnp.sum(jnp.where(diagonal, top[rows], 0.0), axis=0, keepdims=True),
-                        jnp.sum(jnp.where(diagonal, o[rows, HEAD:], 0.0), axis=0, keepdims=True),
-                        jnp.zeros((6, 128), F32),
-                    ],
-                    axis=0,
-                )
-
-    halves = (pl.ds(0, 64), pl.ds(64, 64))
+            see = jnp.concatenate([sight(2 * i), sight(2 * i + 1)], axis=0)
+            parts.append(nt(q, fresh) * SCALE + see)
+            values = jnp.concatenate([values, fresh_v], axis=0)
+        top = parts[0]
+        for p in parts[1:]:
+            top = jnp.maximum(top, p)
+        top = jnp.broadcast_to(jnp.max(top, axis=1, keepdims=True), (256, 128))
+        old = FLOOR if g == 0 else peak[i]
+        top = jnp.maximum(top, old)
+        p = jnp.concatenate([jnp.exp2(p - top).astype(BF16) for p in parts], axis=1)
+        o = mm(p, values)
+        if g > 0:
+            keep = jnp.exp2(old - top)
+            o = o + acc[i] * jnp.concatenate([keep, keep], axis=1)
+        if not last:
+            acc[i] = o
+            peak[i] = top
+            continue
+        for j in range(2):
+            rows = slice(128 * j, 128 * (j + 1))
+            of = (z + ZS[2 * i + j]) % NZ
+            o_send[:, of] = o[rows, :HEAD].astype(BF16).reshape(NZ, 16, HEAD)
+            st_send[pl.ds(of, 1)] = jnp.sum(
+                jnp.where(diagonal, top[rows], 0.0), axis=0, keepdims=True
+            )
+            st_send[pl.ds(NZ + of, 1)] = jnp.sum(
+                jnp.where(diagonal, o[rows, HEAD:], 0.0), axis=0, keepdims=True
+            )
+
+    halves = (pl.ds(0, 4), pl.ds(4, 4))
     rs = [[], []]
     for d in Z_ORDER:
-        to = (z + d) % NZ
-        rs[0].append(send(st_send.at[to], st_recv.at[z], sem_rs, d, dev(dz=d)))
+        rs[0].append(send(st_send, st_recv.at[z], sem_rs, d, dev(dz=d)))
     for half in range(2):
         for d in Z_ORDER:
-            to = (z + d) % NZ
             rs[half].append(
                 send(
-                    o_send.at[to, halves[half]], o_recv.at[z, halves[half]],
+                    o_send.at[(z + d) % NZ, halves[half]], o_recv.at[z, halves[half]],
                     sem_rs, 8 * (half + 1) + d, dev(dz=d),
                 )
             )
     o_recv[z] = o_send[z]
-    st_recv[z] = st_send[z]
+    st_recv[z] = st_send[...]
+    for cp in tz_copies:
+        cp.wait()
+    tt_copies = [send(turn_all.at[:, yx], turn_all.at[:, yx], sem_tt, r, to_yx(r)) for r in YX_ORDER]
     for cp in rs[0]:
         cp.wait()
-    peaks = jnp.concatenate([st_recv[j, 0:1] for j in range(NZ)], axis=0)
-    totals = jnp.concatenate([st_recv[j, 1:2] for j in range(NZ)], axis=0)
+    peaks, totals = st_recv[:, :NZ], st_recv[:, NZ:]
     factor = jnp.exp2(peaks - jnp.max(peaks, axis=0, keepdims=True))
     factor = factor / jnp.sum(factor * totals, axis=0, keepdims=True)
-    factor = jnp.concatenate([factor, jnp.zeros((120, 128), F32)], axis=0).T
+    factors[...] = jnp.concatenate(
+        [factor.reshape(NZ * NZ, 128), jnp.zeros((128 - NZ * NZ, 128), F32)], axis=0
+    ).T
+    factor = factors[pl.ds(pl.multiple_of(16 * z, 16), 16)]
 
     def attended(half):
-        rows = slice(64 * half, 64 * (half + 1))
-        num = 0.0
-        for j in range(NZ):
-            num = num + factor[rows, j : j + 1] * o_recv[j, halves[half]].astype(F32)
-        num = num.reshape(4, 2, ROWS, HEAD)
-        return jnp.concatenate(
-            [num[:, 0].reshape(32, HEAD), num[:, 1].reshape(32, HEAD)], axis=1
-        ).astype(BF16)
+        out = []
+        for of in range(4 * half, 4 * half + 4):
+            num = 0.0
+            for j in range(NZ):
+                at = NZ * j + of
+                num = num + factor[:, at : at + 1] * o_recv[j, of].astype(F32)
+            out.append(jnp.concatenate([num[:ROWS], num[ROWS:]], axis=1))
+        return jnp.concatenate(out, axis=0).astype(BF16)
 
     part_a[0, 0] = attended(0)
     a1 = {r: send(part_a.at[0, 0], part_a.at[0, back_yx(r)], sem_a1, back_yx(r), to_yx(r)) for r in YX_ORDER}
@@ -341,7 +375,7 @@
     ).astype(jnp.int32)
     row, col = iota((16, 1024), 0), iota((16, 1024), 1)
     chosen = (slot_of == 4 * c + row // 4) & (col % 4 == row % 4)
-    every = turn[...].reshape(1024, HEAD)
+    every = turn_all[...].reshape(1024, HEAD)
     kind = col // 8 % 2
     ak_ref[...] = mm((chosen & (kind == 0)).astype(BF16), every).astype(BF16)
     av_ref[...] = mm((chosen & (kind == 1)).astype(BF16), every).astype(BF16)
@@ -383,9 +417,18 @@
     project_a(4)
     to_a = share(sum_a, ha_send, ha_recv, 3)
     finish(sum_b, hb_recv, to_b, 4)
-    for cp in kv_copies + list(a1.values()) + b1 + b2 + a2:
+    for cp in kv_copies + list(q_copies.values()) + list(a1.values()) + b1 + b2 + a2:
         cp.wait_send()
     finish(sum_a, ha_recv, to_a, 0)
+
+
+def write_out(a_in, b_in, c_in, a_out, b_out, c_out, sems):
+    pairs = ((a_in, a_out), (b_in, b_out), (c_in, c_out))
+    copies = [pltpu.make_async_copy(src, dst, sems.at[i]) for i, (src, dst) in enumerate(pairs)]
+    for cp in copies:
+        cp.start()
+    for cp in copies:
+        cp.wait()
 
 
 def on_device(
@@ -395,7 +438,7 @@
     anywhere = pl.BlockSpec(memory_space=pl.ANY)
     vmem = pl.BlockSpec(memory_space=pltpu.VMEM)
     sems = lambda n: pltpu.SemaphoreType.DMA((2, n))
-    layer_out, append_keys, append_values = pl.pallas_call(
+    results = pl.pallas_call(
         kernel,
         out_shape=(
             jax.ShapeDtypeStruct((128, 256), F32),
@@ -406,12 +449,12 @@
         out_specs=(vmem, vmem, vmem),
         scratch_shapes=[
             pltpu.VMEM((128, HEAD), BF16),
-            pltpu.VMEM((NZ, 16, HEAD), BF16),
-            pltpu.VMEM((NZ, NZ, 16, HEAD), BF16),
+            pltpu.VMEM((NZ, 128, HEAD), BF16),
             pltpu.VMEM((NYX, KEYS, HEAD), BF16),
             pltpu.VMEM((NYX, KEYS, HEAD), BF16),
-            pltpu.VMEM((2 * KEYS, 2 * HEAD), BF16),
+            pltpu.VMEM((4, 2 * KEYS, 2 * HEAD), BF16),
             pltpu.VMEM((2048, 256), BF16),
+            pltpu.VMEM((NYX, 16, HEAD), BF16),
             pltpu.VMEM((NZ, NYX, 16, HEAD), BF16),
             pltpu.VMEM((ROWS, HEAD), BF16),
             pltpu.VMEM((ROWS, HEAD), BF16),
@@ -420,10 +463,11 @@
             pltpu.SMEM((NY, 128), jnp.int32),
             pltpu.VMEM((4, 256, 128), F32),
             pltpu.VMEM((4, 256, 256), F32),
-            pltpu.VMEM((NZ, 128, HEAD), BF16),
-            pltpu.VMEM((NZ, 8, 128), F32),
-            pltpu.VMEM((NZ, 128, HEAD), BF16),
-            pltpu.VMEM((NZ, 8, 128), F32),
+            pltpu.VMEM((NZ, NZ, 16, HEAD), BF16),
+            pltpu.VMEM((2 * NZ, 128), F32),
+            pltpu.VMEM((NZ, NZ, 16, HEAD), BF16),
+            pltpu.VMEM((NZ, 2 * NZ, 128), F32),
+            pltpu.VMEM((128, 128), F32),
             pltpu.VMEM((NZ, NYX, 32, 256), BF16),
             pltpu.VMEM((NZ, NYX, 32, 256), BF16),
             pltpu.VMEM((256, 256), F32),
@@ -433,7 +477,7 @@
             pltpu.VMEM((3, 64, 256), BF16),
             pltpu.VMEM((3, 64, 256), BF16),
             pltpu.SemaphoreType.DMA((9,)),
-            sems(8), sems(16), sems(8), sems(8), sems(24), sems(8), sems(8), sems(32), sems(32), sems(6),
+            sems(8), sems(16), sems(8), sems(8), sems(8), sems(24), sems(8), sems(8), sems(32), sems(32), sems(6),
         ],
         compiler_params=pltpu.CompilerParams(
             collective_id=0, has_side_effects=True, vmem_limit_bytes=60 * 1024 * 1024
@@ -450,6 +494,15 @@
         slot_ids.reshape(1, 128),
         block_mask,
     )
+    layer_out, append_keys, append_values = pl.pallas_call(
+        write_out,
+        out_shape=tuple(jax.ShapeDtypeStruct(r.shape, r.dtype) for r in results),
+        in_specs=[anywhere] * 3,
+        out_specs=(anywhere,) * 3,
+        scratch_shapes=[pltpu.SemaphoreType.DMA((3,))],
+        compiler_params=pltpu.CompilerParams(vmem_limit_bytes=60 * 1024 * 1024),
+        name="write_out",
+    )(*results)
     return (
         layer_out,
         append_keys.reshape(16, 1, HEAD),

time: 67.7 us -> 62.7 us (0.926)
  local copies, waits for them, and re-layouts: 2.84 us -> 0 us
  Pallas kernels: 64.1 us -> 62 us
    pallas_call x1, Pallas kernels: 64.1 us -> 56.7 us  [on_device(): pl.pallas_call(kernel, out_shape=(jax.ShapeDtypeStruct((128, 256), F32),...]
    pallas_call x0 -> x1, Pallas kernels: none -> 5.35 us  [on_device(): pl.pallas_call(write_out, out_shape=tuple((jax.ShapeDtypeStruct(r.shape,...]
    unnamed x7 -> x0, local copies, waits for them, and re-layouts: 2.84 us -> none
where the time goes in v3:
time: 62.7 us; the launch traced here: 62.6 us
  Pallas kernels  62 us (99%)
  between operations  0.64 us (1%)
    pallas_call x1, Pallas kernels, on_device(): pl.pallas_call(kernel, out_shape=(jax.ShapeDtypeStruct((128, 256), F32),...  56.7 us
    pallas_call x1, Pallas kernels, on_device(): pl.pallas_call(write_out, out_shape=tuple((jax.ShapeDtypeStruct(r.shape,...  5.35 us

profile of v3, /device:TPU:1, one launch (start us, length us, event | category | flops | bytes accessed | tf_op | source)
XLA Modules:
  0.0 62.6 jit_solution(5852286309706862109)
XLA Ops:
  0.6 56.7 %turn_attention.1 = (f32[128,256]{1,0:T(8,128)}, bf16[16,128]{1,0:T(8,128)(2,1)}, bf16[16,128]{1,0:T(8,128)(2,1)}) custom-call(bf16[128,128]{1,0:T(8,128)(2,1)} %bitcast.11, bf16[256,128]{1,0:T(8,128)(2,1)} %bitcast.9, bf16[256,128]{1,0:T(8,128)(2,1)} %bitcast.10, bf16[2048,256]{1,0:T(8,128)(2,1)} %w_in.1, bf16[8,128]{1,0:T(8,128)(2,1)} %bitcast.12, ...), custom_call_target="tpu_custom_call" | custom-call | tf_op jit(solution)/shard_map/turn_attention/pallas_call | solution.py:441
  57.3 5.3 %write_out.1 = (f32[128,256]{1,0:T(8,128)}, bf16[16,128]{1,0:T(8,128)(2,1)}, bf16[16,128]{1,0:T(8,128)(2,1)}) custom-call(f32[128,256]{1,0:T(8,128)} %get-tuple-element.9.a_in, bf16[16,128]{1,0:T(8,128)(2,1)} %get-tuple-element.10.b_in, bf16[16,128]{1,0:T(8,128)(2,1)} %get-tuple-element.11.c_in), custom_call_target="tpu_custom_call" | custom-call | tf_op jit(solution)/shard_map/write_out/pallas_call | solution.py:497

commit v4 on v3

--- a/solution.py
+++ b/solution.py
@@ -24,9 +24,14 @@
 
 YX = [(0, 0), (0, 1), (1, 0), (1, 1), (3, 0), (3, 1), (2, 0), (2, 1)]
 YX_ORDER = [1, 2, 4, 3, 5, 6, 7]
+YS = [0, 1, 3, 2]
 ZS = [0, 1, 7, 2, 6, 3, 5, 4]
 Z_ORDER = [1, 7, 2, 6, 3, 5, 4]
 Z_BATCHES = [(0, 1), (1, 3), (3, 5), (5, 8)]
+NA = 4
+RA, RB = NA * ROWS, (NZ - NA) * ROWS
+DIRECT = True
+W_PARTS = 4
 KEY_GROUPS = [(0, 1), (2, 4), (6, 3), (5, 7)]
 BLOCKS = [
     (0, 0), (0, 1), (1, 0), (1, 1), (0, 2), (1, 2), (2, 0), (2, 1), (2, 2), (0, 3), (1, 3), (2, 3),
@@ -57,7 +62,7 @@
     q_raw, q_all, k_all, v_all, v_wide, w_all, turn_yx, turn_all, tk, tv, docs_ref, slots_ref, mask_ref,
     peak, acc, o_send, st_send, o_recv, st_recv, factors, part_a, part_b, sum_a, sum_b,
     ha_send, ha_recv, hb_send, hb_recv,
-    sem_in, sem_q, sem_kv, sem_t, sem_tz, sem_tt, sem_rs, sem_a1, sem_b1, sem_a2, sem_b2, sem_h,
+    sem_in, sem_w, sem_q, sem_kv, sem_t, sem_tz, sem_tt, sem_rs, sem_a1, sem_b1, sem_a2, sem_b2, sem_h,
 ):
     c = lax.axis_index("ctx")
     h = lax.axis_index("head")
@@ -67,6 +72,12 @@
     def dev(dy=0, dz=0, dx=0, dh=0):
         ty, tz, tx = (y + dy) % NY, (z + dz) % NZ, (x + dx) % NX
         return ((ty * NZ + tz) * NX + tx, (h + dh) % NH)
+
+    def to_y(i):
+        return dev(dy=YS[i])
+
+    def back_y(i):
+        return YS.index((NY - YS[i]) % NY)
 
     def to_yx(r):
         return dev(dy=YX[r][0], dx=YX[r][1])
@@ -87,29 +98,19 @@
         copy.start()
         return copy
 
+    barrier = pltpu.get_barrier_semaphore()
+    peers = [to_yx(r) for r in YX_ORDER] + [dev(dz=d) for d in Z_ORDER]
+    peers += [dev(dx=dx, dh=d) for dx in range(NX) for d in range(1, NH)]
+    for p in peers:
+        pl.semaphore_signal(barrier, inc=1, device_id=p, device_id_type=MESH)
+
     get_q = fetch(q_in, q_raw, 0)
     get_small = [
         fetch(tk_in, tk, 1), fetch(tv_in, tv, 2), fetch(doc_in, docs_ref, 3),
         fetch(slot_in, slots_ref, 4), fetch(mask_in, mask_ref, 5),
     ]
     get_kv = [fetch(ck_in, k_all.at[0], 6), fetch(cv_in, v_all.at[0], 7)]
-    get_w = fetch(w_in, w_all, 8)
-
-    barrier = pltpu.get_barrier_semaphore()
-    peers = [to_yx(r) for r in YX_ORDER] + [dev(dz=d) for d in Z_ORDER]
-    peers += [dev(dh=d) for d in range(1, NH)]
-    for p in peers:
-        pl.semaphore_signal(barrier, inc=1, device_id=p, device_id_type=MESH)
-
-    get_q.wait()
-    i0, i1 = iota((128, 128), 0), iota((128, 128), 1)
-    order = (i1 == (i0 % ROWS) * GROUP + i0 // ROWS).astype(BF16)
-    q_all[0] = mm(order, q_raw[...]).astype(BF16)
-    for cp in get_small:
-        cp.wait()
-    mine = jnp.concatenate([tk[...].astype(F32), tv[...].astype(F32)], axis=0).astype(BF16)
-    turn_yx[yx] = mine
-    turn_all[z, yx] = mine
+    get_w = fetch(w_in, w_all.at[0], 8)
 
     pl.semaphore_wait(barrier, len(peers))
 
@@ -119,13 +120,23 @@
     def give_v(src, slot, device):
         return send(src, v_all.at[slot], sem_kv, 2 * slot + 1, device)
 
-    q_copies = {d: send(q_all.at[0], q_all.at[ZS.index(NZ - d)], sem_q, ZS.index(NZ - d), dev(dz=d)) for d in Z_ORDER}
     kv_copies = [give_v(cv_in, 1, to_yx(1))]
     for r in (2, 4, 6):
         kv_copies.append(give_k(ck_in, back_yx(r), to_yx(r)))
     kv_copies.append(give_k(ck_in, 1, to_yx(1)))
     for r in (2, 4, 6):
         kv_copies.append(give_v(cv_in, back_yx(r), to_yx(r)))
+
+    get_q.wait()
+    i0, i1 = iota((128, 128), 0), iota((128, 128), 1)
+    order = (i1 == (i0 % ROWS) * GROUP + i0 // ROWS).astype(BF16)
+    q_all[0] = mm(order, q_raw[...]).astype(BF16)
+    q_copies = {d: send(q_all.at[0], q_all.at[ZS.index(NZ - d)], sem_q, ZS.index(NZ - d), dev(dz=d)) for d in Z_ORDER}
+    for cp in get_small:
+        cp.wait()
+    mine = jnp.concatenate([tk[...].astype(F32), tv[...].astype(F32)], axis=0).astype(BF16)
+    turn_yx[yx] = mine
+    turn_all[z, yx] = mine
     t_copies = [send(turn_yx.at[yx], turn_yx.at[yx], sem_t, r, to_yx(r)) for r in YX_ORDER]
     tz_copies = [send(turn_yx.at[yx], turn_all.at[z, yx], sem_tz, d, dev(dz=d)) for d in Z_ORDER]
 
@@ -161,6 +172,11 @@
     for r in (2, 4, 6):
         arrived(k_all.at[r], sem_kv, 2 * r)
         kv_copies.append(give_k(k_all.at[r], r + 1, to_yx(1)))
+    w_rows = 2048 // W_PARTS
+    w_copies = []
+    for i in range(W_PARTS):
+        rows = pl.ds(w_rows * i, w_rows)
+        w_copies.append(send(w_in.at[rows], w_all.at[1, rows], sem_w, i, dev(dx=1)))
 
     have = {("k", 2), ("k", 4), ("k", 6), ("v", 1)}
     biases = {}
@@ -231,7 +247,7 @@
                 jnp.where(diagonal, o[rows, HEAD:], 0.0), axis=0, keepdims=True
             )
 
-    halves = (pl.ds(0, 4), pl.ds(4, 4))
+    halves = (pl.ds(0, NA), pl.ds(NA, NZ - NA))
     rs = [[], []]
     for d in Z_ORDER:
         rs[0].append(send(st_send, st_recv.at[z], sem_rs, d, dev(dz=d)))
@@ -260,7 +276,7 @@
 
     def attended(half):
         out = []
-        for of in range(4 * half, 4 * half + 4):
+        for of in (range(NA), range(NA, NZ))[half]:
             num = 0.0
             for j in range(NZ):
                 at = NZ * j + of
@@ -269,7 +285,23 @@
         return jnp.concatenate(out, axis=0).astype(BF16)
 
     part_a[0, 0] = attended(0)
-    a1 = {r: send(part_a.at[0, 0], part_a.at[0, back_yx(r)], sem_a1, back_yx(r), to_yx(r)) for r in YX_ORDER}
+    a1 = [
+        send(part_a.at[0, 0], part_a.at[0, back_y(i)], sem_a1, back_y(i), to_y(i)) for i in (1, 2, 3)
+    ]
+    a2, b2 = [], []
+
+    def give(slot, i, steps):
+        for step in steps:
+            dst = (slot - step) % NZ
+            if dst != 4 or (step > 0) == (i < NY // 2):
+                a2.append(
+                    send(part_a.at[slot, i], part_a.at[dst, i], sem_a2, NZ * i + dst, dev(dz=step))
+                )
+
+    def got(slot, i):
+        arrived(part_a.at[slot, i], sem_a2, NZ * i + slot)
+
+    give(0, 0, (1, -1, 2, -2))
     for cp in rs[1]:
         cp.wait()
     part_b[0, 0] = attended(1)
@@ -277,93 +309,63 @@
         send(part_b.at[0, 0], part_b.at[ZS.index(NZ - d), 0], sem_b1, ZS.index(NZ - d), dev(dz=d))
         for d in Z_ORDER
     ]
-    b2, a2 = [], []
 
     def spread(batch):
         lo, hi = Z_BATCHES[batch]
         for s in range(lo, hi):
             if s:
                 arrived(part_b.at[s, 0], sem_b1, s)
-        for r in YX_ORDER:
-            b = back_yx(r)
+        for i in (1, 2, 3):
+            b = back_y(i)
             b2.append(
                 send(
                     part_b.at[pl.ds(lo, hi - lo), 0], part_b.at[pl.ds(lo, hi - lo), b],
-                    sem_b2, 8 * batch + b, to_yx(r),
+                    sem_b2, 4 * batch + b, to_y(i),
                 )
             )
 
     def spread_arrived(batch):
         lo, hi = Z_BATCHES[batch]
-        for r in YX_ORDER:
-            arrived(part_b.at[pl.ds(lo, hi - lo), r], sem_b2, 8 * batch + r)
-
-    def piece(slot, p):
-        return part_a.at[slot, pl.ds(2 * p, 2)]
-
-    def index(hop, way, p):
-        return 8 * hop + 4 * way + p
-
-    def pass_on(hop, p, both=True):
-        for way, (step, src, dst) in enumerate((
-            (1, (NZ - hop) % NZ, NZ - 1 - hop), (-1, hop, hop + 1),
-        )):
-            if hop == 3:
-                if p // 2 != way:
-                    continue
-                step, src, dst = 2 * step, (6, 2)[way], 4
-            a2.append(send(piece(src, p), piece(dst, p), sem_a2, index(hop, way, p), dev(dz=step)))
-
-    def passed(hop, p):
-        for way in range(2):
-            dst = (NZ - 1 - hop, hop + 1)[way]
-            if hop == 3:
-                if p // 2 != way:
-                    continue
-                dst = 4
-            arrived(piece(dst, p), sem_a2, index(hop, way, p))
-
-    def weight(dz):
+        for i in (1, 2, 3):
+            arrived(part_b.at[pl.ds(lo, hi - lo), i], sem_b2, 4 * batch + i)
+
+    def project(part, total, slot, dz, columns):
         at = pl.multiple_of((z + dz) % NZ * 256, 256)
-        return w_all[pl.ds(at, 256)]
-
-    def project_a(slot):
-        part = mm(part_a[slot].reshape(256, 256), weight(slot))
-        sum_a[...] = part if slot == 0 else sum_a[...] + part
-
-    def project_b(batch):
-        lo, hi = Z_BATCHES[batch]
-        part = 0.0
-        for s in range(lo, hi):
-            part = part + mm(part_b[s].reshape(256, 256), weight(ZS[s]))
-        sum_b[...] = part if batch == 0 else sum_b[...] + part
+        size = part.shape[1] * part.shape[2]
+        new = mm(part[slot].reshape(size, 256), w_all[columns, pl.ds(at, 256)])
+        total[columns] = new if dz == 0 else total[columns] + new
+
+    def project_a(slots, columns):
+        for slot in slots:
+            project(part_a, sum_a, slot, slot, columns)
+
+    def project_b(batches, columns):
+        for batch in batches:
+            for s in range(*Z_BATCHES[batch]):
+                project(part_b, sum_b, s, ZS[s], columns)
 
     spread(0)
-    for p in range(4):
-        for r in (2 * p, 2 * p + 1):
-            if r:
-                arrived(part_a.at[0, r], sem_a1, r)
-        pass_on(0, p)
-        if p == 1:
+    for i in (1, 2, 3):
+        arrived(part_a.at[0, i], sem_a1, i)
+        give(0, i, (1, -1, 2, -2))
+        if i == 2:
             spread(1)
     spread(2)
     get_w.wait()
-    project_a(0)
-    for p in range(4):
-        passed(0, p)
-        pass_on(1, p)
-        if p == 0:
+    project_a((0,), 0)
+    for i in range(NY):
+        got(6, i)
+        give(6, i, (1, 2))
+        got(2, i)
+        give(2, i, (-1, -2))
+        if i == 0:
             spread(3)
-    spread_arrived(0)
-    project_a(1)
-    project_a(7)
-    project_b(0)
-    for p in range(4):
-        passed(1, p)
-        pass_on(2, p)
-        pass_on(3, p)
-    project_a(2)
-    project_a(6)
+        got(1, i)
+        got(7, i)
+    project_a((1, 7, 2, 6), 0)
+    for batch in range(3):
+        spread_arrived(batch)
+        project_b((batch,), 0)
 
     for cp in tt_copies:
         cp.wait()
@@ -380,54 +382,64 @@
     ak_ref[...] = mm((chosen & (kind == 0)).astype(BF16), every).astype(BF16)
     av_ref[...] = mm((chosen & (kind == 1)).astype(BF16), every).astype(BF16)
 
-    def rows_of(head):
+    for cp in w_copies:
+        cp.wait()
+    project_a((0, 1, 7, 2, 6), 1)
+    project_b((0, 1, 2), 1)
+
+    def rows_of(head, size):
         dy = (head + NY - y) % NY
-        return pl.ds(pl.multiple_of(64 * jnp.where(dy >= 2, 5 - dy, dy), 64), 64)
-
-    def share(total, sent, got, base):
+        return pl.ds(pl.multiple_of(size * jnp.where(dy >= 2, 5 - dy, dy), size), size)
+
+    def share(total, sent, got, base, size):
         copies = []
-        for d in (2, 3, 1):
-            sent[d - 1] = total[rows_of((h + d) % NH)].astype(BF16)
-            copies.append(send(sent.at[d - 1], got.at[3 - d], sem_h, base + 3 - d, dev(dh=d)))
+        for columns, d in ((0, 2), (1, 2), (0, 3), (1, 3), (0, 1), (1, 1), (1, 0)):
+            slot = NH * columns + d
+            back = NH * columns + (NH - d) % NH
+            sent[slot] = total[columns, rows_of((h + d) % NH, size)].astype(BF16)
+            copies.append(
+                send(sent.at[slot], got.at[back], sem_h, base + back, dev(dx=columns, dh=d))
+            )
         return copies
 
-    def finish(total, got, copies, first):
+    def finish(total, got, copies, first, size):
         for cp in copies:
             cp.wait()
-        whole = total[rows_of(h)]
-        for j in range(3):
-            whole = whole + got[j].astype(F32)
-        for dx in range(NX):
-            for j in range(4):
-                at = 16 * (first + j) + 8 * ((x + dx) % NX)
-                out_ref[pl.ds(pl.multiple_of(at, 8), 8)] = whole[
-                    32 * dx + 8 * j : 32 * dx + 8 * j + 8
-                ]
-
-    for batch in range(1, 4):
-        spread_arrived(batch)
-        project_b(batch)
-    to_b = share(sum_b, hb_send, hb_recv, 0)
-    for p in range(4):
-        passed(2, p)
-    project_a(3)
-    project_a(5)
-    for p in range(4):
-        passed(3, p)
-    project_a(4)
-    to_a = share(sum_a, ha_send, ha_recv, 3)
-    finish(sum_b, hb_recv, to_b, 4)
-    for cp in kv_copies + list(q_copies.values()) + list(a1.values()) + b1 + b2 + a2:
+        whole = [total[0, rows_of(h, size)], got[NH].astype(F32)]
+        for columns in range(2):
+            for d in range(1, NH):
+                whole[columns] = whole[columns] + got[NH * columns + d].astype(F32)
+            for j in range(size // ROWS):
+                at = 16 * (first + j) + 8 * ((x + columns) % NX)
+                out_ref[pl.ds(pl.multiple_of(at, 8), 8)] = whole[columns][8 * j : 8 * j + 8]
+
+    spread_arrived(3)
+    project_b((3,), 0)
+    project_b((3,), 1)
+    to_b = share(sum_b, hb_send, hb_recv, 0, RB)
+    for slot in (3, 5, 4):
+        for i in range(NY):
+            got(slot, i)
+        project_a((slot,), 0)
+        project_a((slot,), 1)
+    to_a = share(sum_a, ha_send, ha_recv, 8, RA)
+    finish(sum_b, hb_recv, to_b, NA, RB)
+    for cp in kv_copies + list(q_copies.values()) + a1 + b1 + b2 + a2:
         cp.wait_send()
-    finish(sum_a, ha_recv, to_a, 0)
-
-
-def write_out(a_in, b_in, c_in, a_out, b_out, c_out, sems):
-    pairs = ((a_in, a_out), (b_in, b_out), (c_in, c_out))
-    copies = [pltpu.make_async_copy(src, dst, sems.at[i]) for i, (src, dst) in enumerate(pairs)]
-    for cp in copies:
+    finish(sum_a, ha_recv, to_a, 0, RA)
+
+
+def write_out(a_in, b_in, c_in, a_out, b_out, c_out, a_mid, b_mid, c_mid, sems):
+    ins = [(a_in, a_mid), (b_in, b_mid), (c_in, c_mid)]
+    outs = [(a_mid, a_out), (b_mid, b_out), (c_mid, c_out)]
+    ins = [pltpu.make_async_copy(*pair, sems.at[0, i]) for i, pair in enumerate(ins)]
+    outs = [pltpu.make_async_copy(*pair, sems.at[1, i]) for i, pair in enumerate(outs)]
+    for cp in ins:
         cp.start()
-    for cp in copies:
+    for i in (1, 2, 0):
+        ins[i].wait()
+        outs[i].start()
+    for cp in outs:
         cp.wait()
 
 
@@ -453,7 +465,7 @@
             pltpu.VMEM((NYX, KEYS, HEAD), BF16),
             pltpu.VMEM((NYX, KEYS, HEAD), BF16),
             pltpu.VMEM((4, 2 * KEYS, 2 * HEAD), BF16),
-            pltpu.VMEM((2048, 256), BF16),
+            pltpu.VMEM((NX, 2048, 256), BF16),
             pltpu.VMEM((NYX, 16, HEAD), BF16),
             pltpu.VMEM((NZ, NYX, 16, HEAD), BF16),
             pltpu.VMEM((ROWS, HEAD), BF16),
@@ -468,16 +480,17 @@
             pltpu.VMEM((NZ, NZ, 16, HEAD), BF16),
             pltpu.VMEM((NZ, 2 * NZ, 128), F32),
             pltpu.VMEM((128, 128), F32),
-            pltpu.VMEM((NZ, NYX, 32, 256), BF16),
-            pltpu.VMEM((NZ, NYX, 32, 256), BF16),
-            pltpu.VMEM((256, 256), F32),
-            pltpu.VMEM((256, 256), F32),
-            pltpu.VMEM((3, 64, 256), BF16),
-            pltpu.VMEM((3, 64, 256), BF16),
-            pltpu.VMEM((3, 64, 256), BF16),
-            pltpu.VMEM((3, 64, 256), BF16),
+            pltpu.VMEM((NZ, NY, RA, 256), BF16),
+            pltpu.VMEM((NZ, NY, RB, 256), BF16),
+            pltpu.VMEM((NX, NY * RA, 256), F32),
+            pltpu.VMEM((NX, NY * RB, 256), F32),
+            pltpu.VMEM((2 * NH, RA, 256), BF16),
+            pltpu.VMEM((2 * NH, RA, 256), BF16),
+            pltpu.VMEM((2 * NH, RB, 256), BF16),
+            pltpu.VMEM((2 * NH, RB, 256), BF16),
             pltpu.SemaphoreType.DMA((9,)),
-            sems(8), sems(16), sems(8), sems(8), sems(8), sems(24), sems(8), sems(8), sems(32), sems(32), sems(6),
+            sems(W_PARTS), sems(8), sems(16), sems(8), sems(8), sems(8), sems(24), sems(4), sems(8), sems(32),
+            sems(16), sems(16),
         ],
         compiler_params=pltpu.CompilerParams(
             collective_id=0, has_side_effects=True, vmem_limit_bytes=60 * 1024 * 1024
@@ -499,7 +512,8 @@
         out_shape=tuple(jax.ShapeDtypeStruct(r.shape, r.dtype) for r in results),
         in_specs=[anywhere] * 3,
         out_specs=(anywhere,) * 3,
-        scratch_shapes=[pltpu.SemaphoreType.DMA((3,))],
+        scratch_shapes=[pltpu.VMEM(r.shape, r.dtype) for r in results]
+        + [pltpu.SemaphoreType.DMA((2, 3))],
         compiler_params=pltpu.CompilerParams(vmem_limit_bytes=60 * 1024 * 1024),
         name="write_out",
     )(*results)

time: 62.7 us -> 57.9 us (0.923)
  Pallas kernels: 62 us -> 57.1 us
    pallas_call x1, Pallas kernels: 5.35 us -> 1.62 us  [on_device(): pl.pallas_call(write_out, out_shape=tuple((jax.ShapeDtypeStruct(r.shape,...]
    pallas_call x1, Pallas kernels: 56.7 us -> 55.5 us  [on_device(): pl.pallas_call(kernel, out_shape=(jax.ShapeDtypeStruct((128, 256), F32),...]
where the time goes in v4:
time: 57.9 us; the launch traced here: 57.8 us
  Pallas kernels  57.1 us (99%)
  between operations  0.64 us (1%)
    pallas_call x1, Pallas kernels, on_device(): pl.pallas_call(kernel, out_shape=(jax.ShapeDtypeStruct((128, 256), F32),...  55.5 us
    pallas_call x1, Pallas kernels, on_device(): pl.pallas_call(write_out, out_shape=tuple((jax.ShapeDtypeStruct(r.shape,...  1.62 us

profile of v4, /device:TPU:1, one launch (start us, length us, event | category | flops | bytes accessed | tf_op | source)
XLA Modules:
  0.0 57.8 jit_solution(1769753275015606147)
XLA Ops:
  0.6 55.5 %turn_attention.1 = (f32[128,256]{1,0:T(8,128)}, bf16[16,128]{1,0:T(8,128)(2,1)}, bf16[16,128]{1,0:T(8,128)(2,1)}) custom-call(bf16[128,128]{1,0:T(8,128)(2,1)} %bitcast.11, bf16[256,128]{1,0:T(8,128)(2,1)} %bitcast.9, bf16[256,128]{1,0:T(8,128)(2,1)} %bitcast.10, bf16[2048,256]{1,0:T(8,128)(2,1)} %w_in.1, bf16[8,128]{1,0:T(8,128)(2,1)} %bitcast.12, ...), custom_call_target="tpu_custom_call" | custom-call | tf_op jit(solution)/shard_map/turn_attention/pallas_call | solution.py:453
  56.2 1.6 %write_out.1 = (f32[128,256]{1,0:T(8,128)}, bf16[16,128]{1,0:T(8,128)(2,1)}, bf16[16,128]{1,0:T(8,128)(2,1)}) custom-call(f32[128,256]{1,0:T(8,128)} %get-tuple-element.9.a_in, bf16[16,128]{1,0:T(8,128)(2,1)} %get-tuple-element.10.b_in, bf16[16,128]{1,0:T(8,128)(2,1)} %get-tuple-element.11.c_in), custom_call_target="tpu_custom_call" | custom-call | tf_op jit(solution)/shard_map/write_out/pallas_call | solution.py:510

commit v5 on v4

--- a/solution.py
+++ b/solution.py
@@ -27,11 +27,18 @@
 YS = [0, 1, 3, 2]
 ZS = [0, 1, 7, 2, 6, 3, 5, 4]
 Z_ORDER = [1, 7, 2, 6, 3, 5, 4]
-Z_BATCHES = [(0, 1), (1, 3), (3, 5), (5, 8)]
+Z_BATCHES = [(0, 1), (1, 3), (3, 5), (5, 7), (7, 8)]
 NA = 4
 RA, RB = NA * ROWS, (NZ - NA) * ROWS
 DIRECT = True
-W_PARTS = 4
+SENT = [
+    "q", "k", "v", "t", "tz", "tt", "st", "rs0", "rs1", "a1", "b1", "a2", "b2", "ha", "hb", "w",
+]
+GOT = [
+    "q0", "q1", "q2", "q3", "v1", "k1", "k2", "k4", "k6", "g1", "g2", "g3", "t", "tz", "tt", "st",
+    "rs0", "rs1", "a1_1", "a1_2", "a1_3", "b1_1", "b1_2", "b1_3", "b1_4", "a2_0", "a2_1", "a2_2",
+    "a2_3", "a2_side", "a2_far", "b2_0", "b2_1", "b2_2", "b2_3", "b2_4", "ha", "hb", "w",
+]
 KEY_GROUPS = [(0, 1), (2, 4), (6, 3), (5, 7)]
 BLOCKS = [
     (0, 0), (0, 1), (1, 0), (1, 1), (0, 2), (1, 2), (2, 0), (2, 1), (2, 2), (0, 3), (1, 3), (2, 3),
@@ -58,11 +65,11 @@
 
 def kernel(
     q_in, ck_in, cv_in, w_in, tk_in, tv_in, doc_in, slot_in, mask_in,
-    out_ref, ak_ref, av_ref,
+    out_hbm, ak_hbm, av_hbm,
     q_raw, q_all, k_all, v_all, v_wide, w_all, turn_yx, turn_all, tk, tv, docs_ref, slots_ref, mask_ref,
-    peak, acc, o_send, st_send, o_recv, st_recv, factors, part_a, part_b, sum_a, sum_b,
-    ha_send, ha_recv, hb_send, hb_recv,
-    sem_in, sem_w, sem_q, sem_kv, sem_t, sem_tz, sem_tt, sem_rs, sem_a1, sem_b1, sem_a2, sem_b2, sem_h,
+    peak, acc, o_send, st_send, o_recv, st_recv, factors, wide, sights, part_a, part_b, sum_a, sum_b,
+    ha_send, ha_recv, hb_send, hb_recv, out_ref, ak_ref, av_ref,
+    sem_in, sem_out, sem_sent, sem_got,
 ):
     c = lax.axis_index("ctx")
     h = lax.axis_index("head")
@@ -82,16 +89,22 @@
     def to_yx(r):
         return dev(dy=YX[r][0], dx=YX[r][1])
 
-    def send(src, dst, sems, i, device):
-        copy = pltpu.make_async_remote_copy(
-            src_ref=src, dst_ref=dst, send_sem=sems.at[0, i], recv_sem=sems.at[1, i],
-            device_id=device, device_id_type=MESH,
-        )
+    def send(src, dst, sent, got, device):
+        pltpu.make_async_remote_copy(
+            src_ref=src, dst_ref=dst, send_sem=sem_sent.at[SENT.index(sent)],
+            recv_sem=sem_got.at[GOT.index(got)], device_id=device, device_id_type=MESH,
+        ).start()
+
+    def arrived(ref, got):
+        pltpu.make_async_copy(ref, ref, sem_got.at[GOT.index(got)]).wait()
+
+    def left(ref, sent):
+        pltpu.make_async_copy(ref, ref, sem_sent.at[SENT.index(sent)]).wait()
+
+    def put(src, dst, i):
+        copy = pltpu.make_async_copy(src, dst, sem_out.at[i])
         copy.start()
         return copy
-
-    def arrived(ref, sems, i):
-        pltpu.make_async_copy(ref, ref, sems.at[1, i]).wait()
 
     def fetch(src, dst, i):
         copy = pltpu.make_async_copy(src, dst, sem_in.at[i])
@@ -115,30 +128,36 @@
     pl.semaphore_wait(barrier, len(peers))
 
     def give_k(src, slot, device):
-        return send(src, k_all.at[slot], sem_kv, 2 * slot, device)
+        got = f"k{slot}" if slot in (1, 2, 4, 6) else ("g2" if slot == 3 else "g3")
+        send(src, k_all.at[slot], "k", got, device)
 
     def give_v(src, slot, device):
-        return send(src, v_all.at[slot], sem_kv, 2 * slot + 1, device)
-
-    kv_copies = [give_v(cv_in, 1, to_yx(1))]
+        got = {1: "v1", 2: "g1", 4: "g1", 3: "g2", 6: "g2"}.get(slot, "g3")
+        send(src, v_all.at[slot], "v", got, device)
+
+    give_v(cv_in, 1, to_yx(1))
     for r in (2, 4, 6):
-        kv_copies.append(give_k(ck_in, back_yx(r), to_yx(r)))
-    kv_copies.append(give_k(ck_in, 1, to_yx(1)))
+        give_k(ck_in, back_yx(r), to_yx(r))
+    give_k(ck_in, 1, to_yx(1))
     for r in (2, 4, 6):
-        kv_copies.append(give_v(cv_in, back_yx(r), to_yx(r)))
+        give_v(cv_in, back_yx(r), to_yx(r))
 
     get_q.wait()
     i0, i1 = iota((128, 128), 0), iota((128, 128), 1)
     order = (i1 == (i0 % ROWS) * GROUP + i0 // ROWS).astype(BF16)
     q_all[0] = mm(order, q_raw[...]).astype(BF16)
-    q_copies = {d: send(q_all.at[0], q_all.at[ZS.index(NZ - d)], sem_q, ZS.index(NZ - d), dev(dz=d)) for d in Z_ORDER}
+    for d in Z_ORDER:
+        slot = ZS.index(NZ - d)
+        send(q_all.at[0], q_all.at[slot], "q", f"q{slot // 2}", dev(dz=d))
     for cp in get_small:
         cp.wait()
     mine = jnp.concatenate([tk[...].astype(F32), tv[...].astype(F32)], axis=0).astype(BF16)
     turn_yx[yx] = mine
     turn_all[z, yx] = mine
-    t_copies = [send(turn_yx.at[yx], turn_yx.at[yx], sem_t, r, to_yx(r)) for r in YX_ORDER]
-    tz_copies = [send(turn_yx.at[yx], turn_all.at[z, yx], sem_tz, d, dev(dz=d)) for d in Z_ORDER]
+    for r in YX_ORDER:
+        send(turn_yx.at[yx], turn_yx.at[yx], "t", "t", to_yx(r))
+    for d in Z_ORDER:
+        send(turn_yx.at[yx], turn_all.at[z, yx], "tz", "tz", dev(dz=d))
 
     docs = docs_ref[...]
     key_token = 16 * z + 8 * (i1 // 16 % 2) + i1 % 8
@@ -166,32 +185,27 @@
 
     diagonal = i0 == i1
 
-    arrived(v_all.at[1], sem_kv, 3)
+    arrived(v_all.at[1], "v1")
     for r in (2, 4, 6):
-        kv_copies.append(give_v(v_all.at[1], back_yx(r + 1), to_yx(r)))
+        give_v(v_all.at[1], back_yx(r + 1), to_yx(r))
+    for slot in range(NZ):
+        sights[slot] = sight(slot)
     for r in (2, 4, 6):
-        arrived(k_all.at[r], sem_kv, 2 * r)
-        kv_copies.append(give_k(k_all.at[r], r + 1, to_yx(1)))
-    w_rows = 2048 // W_PARTS
-    w_copies = []
-    for i in range(W_PARTS):
-        rows = pl.ds(w_rows * i, w_rows)
-        w_copies.append(send(w_in.at[rows], w_all.at[1, rows], sem_w, i, dev(dx=1)))
-
-    have = {("k", 2), ("k", 4), ("k", 6), ("v", 1)}
+        arrived(k_all.at[r], f"k{r}")
+        give_k(k_all.at[r], r + 1, to_yx(1))
+    send(w_in, w_all.at[1], "w", "w", dev(dx=1))
+
     biases = {}
     for g, i in BLOCKS:
         last = g == 3
         if i == 0:
+            if g == 0:
+                for cp in get_kv:
+                    cp.wait()
+                arrived(k_all.at[1], "k1")
+            else:
+                arrived(k_all.at[pl.ds(0, g + 1)], f"g{g}")
             for j, r in enumerate(KEY_GROUPS[g]):
-                if r == 0:
-                    for cp in get_kv:
-                        cp.wait()
-                else:
-                    if ("k", r) not in have:
-                        arrived(k_all.at[r], sem_kv, 2 * r)
-                    if ("v", r) not in have:
-                        arrived(v_all.at[r], sem_kv, 2 * r + 1)
                 v_wide[g, KEYS * j : KEYS * (j + 1), :HEAD] = v_all[r]
             v_wide[g, :, HEAD:] = jnp.ones((2 * KEYS, HEAD), BF16)
             biases[g] = []
@@ -199,16 +213,13 @@
                 source = ((y + YX[r][0]) % NY * NZ + z) * NX + (x + YX[r][1]) % NX
                 for b in range(2):
                     biases[g].append(jnp.where(mask_ref[y, 2 * source + b] == 1, 0.0, NEG))
-            if last:
-                for cp in t_copies:
-                    cp.wait()
+            if g == 1:
+                arrived(turn_yx.at[pl.ds(1, NYX - 1)], "t")
                 fresh = turn_yx[...].reshape(128, HEAD)
                 fresh_v = mm((i1 == i0 + 8).astype(BF16), fresh).astype(BF16)
                 fresh_v = jnp.concatenate([fresh_v, jnp.ones((128, HEAD), BF16)], axis=1)
         if g == 0:
-            for slot in (2 * i, 2 * i + 1):
-                if slot:
-                    arrived(q_all.at[slot], sem_q, slot)
+            arrived(q_all.at[pl.ds(2 * i, 2)] if i else q_all.at[1], f"q{i}")
         q = q_all[2 * i : 2 * i + 2].reshape(256, HEAD)
         parts = []
         for j, r in enumerate(KEY_GROUPS[g]):
@@ -217,9 +228,8 @@
                 s[:, :128] * SCALE + biases[g][2 * j], s[:, 128:] * SCALE + biases[g][2 * j + 1]
             ]
         values = v_wide[g]
-        if last:
-            see = jnp.concatenate([sight(2 * i), sight(2 * i + 1)], axis=0)
-            parts.append(nt(q, fresh) * SCALE + see)
+        if g == 1:
+            parts.append(nt(q, fresh) * SCALE + sights[2 * i : 2 * i + 2].reshape(256, 128))
             values = jnp.concatenate([values, fresh_v], axis=0)
         top = parts[0]
         for p in parts[1:]:
@@ -248,24 +258,21 @@
             )
 
     halves = (pl.ds(0, NA), pl.ds(NA, NZ - NA))
-    rs = [[], []]
     for d in Z_ORDER:
-        rs[0].append(send(st_send, st_recv.at[z], sem_rs, d, dev(dz=d)))
+        send(st_send, st_recv.at[z], "st", "st", dev(dz=d))
     for half in range(2):
         for d in Z_ORDER:
-            rs[half].append(
-                send(
-                    o_send.at[(z + d) % NZ, halves[half]], o_recv.at[z, halves[half]],
-                    sem_rs, 8 * (half + 1) + d, dev(dz=d),
-                )
+            send(
+                o_send.at[(z + d) % NZ, halves[half]], o_recv.at[z, halves[half]],
+                f"rs{half}", f"rs{half}", dev(dz=d),
             )
     o_recv[z] = o_send[z]
     st_recv[z] = st_send[...]
-    for cp in tz_copies:
-        cp.wait()
-    tt_copies = [send(turn_all.at[:, yx], turn_all.at[:, yx], sem_tt, r, to_yx(r)) for r in YX_ORDER]
-    for cp in rs[0]:
-        cp.wait()
+    others = pl.ds(1, NZ - 1)
+    arrived(turn_all.at[others, 0], "tz")
+    for r in YX_ORDER:
+        send(turn_all.at[:, yx], turn_all.at[:, yx], "tt", "tt", to_yx(r))
+    arrived(st_recv.at[others], "st")
     peaks, totals = st_recv[:, :NZ], st_recv[:, NZ:]
     factor = jnp.exp2(peaks - jnp.max(peaks, axis=0, keepdims=True))
     factor = factor / jnp.sum(factor * totals, axis=0, keepdims=True)
@@ -273,61 +280,49 @@
         [factor.reshape(NZ * NZ, 128), jnp.zeros((128 - NZ * NZ, 128), F32)], axis=0
     ).T
     factor = factors[pl.ds(pl.multiple_of(16 * z, 16), 16)]
+    for at in range(NZ * NZ):
+        wide[at] = jnp.broadcast_to(factor[:, at : at + 1], (16, HEAD))
 
     def attended(half):
         out = []
         for of in (range(NA), range(NA, NZ))[half]:
             num = 0.0
             for j in range(NZ):
-                at = NZ * j + of
-                num = num + factor[:, at : at + 1] * o_recv[j, of].astype(F32)
+                num = num + wide[NZ * j + of] * o_recv[j, of].astype(F32)
             out.append(jnp.concatenate([num[:ROWS], num[ROWS:]], axis=1))
         return jnp.concatenate(out, axis=0).astype(BF16)
 
+    arrived(o_recv.at[others, halves[0]], "rs0")
     part_a[0, 0] = attended(0)
-    a1 = [
-        send(part_a.at[0, 0], part_a.at[0, back_y(i)], sem_a1, back_y(i), to_y(i)) for i in (1, 2, 3)
-    ]
-    a2, b2 = [], []
+    for i in (1, 2, 3):
+        send(part_a.at[0, 0], part_a.at[0, back_y(i)], "a1", f"a1_{back_y(i)}", to_y(i))
 
     def give(slot, i, steps):
         for step in steps:
             dst = (slot - step) % NZ
             if dst != 4 or (step > 0) == (i < NY // 2):
-                a2.append(
-                    send(part_a.at[slot, i], part_a.at[dst, i], sem_a2, NZ * i + dst, dev(dz=step))
-                )
-
-    def got(slot, i):
-        arrived(part_a.at[slot, i], sem_a2, NZ * i + slot)
+                got = f"a2_{i}" if dst in (2, 6) else ("a2_side" if dst in (1, 7) else "a2_far")
+                send(part_a.at[slot, i], part_a.at[dst, i], "a2", got, dev(dz=step))
 
     give(0, 0, (1, -1, 2, -2))
-    for cp in rs[1]:
-        cp.wait()
+    arrived(o_recv.at[others, halves[1]], "rs1")
     part_b[0, 0] = attended(1)
-    b1 = [
-        send(part_b.at[0, 0], part_b.at[ZS.index(NZ - d), 0], sem_b1, ZS.index(NZ - d), dev(dz=d))
-        for d in Z_ORDER
-    ]
+    batch_of = {s: k for k, (lo, hi) in enumerate(Z_BATCHES) for s in range(lo, hi)}
+    for d in Z_ORDER:
+        slot = ZS.index(NZ - d)
+        send(part_b.at[0, 0], part_b.at[slot, 0], "b1", f"b1_{batch_of[slot]}", dev(dz=d))
 
     def spread(batch):
         lo, hi = Z_BATCHES[batch]
-        for s in range(lo, hi):
-            if s:
-                arrived(part_b.at[s, 0], sem_b1, s)
+        slots = pl.ds(lo, hi - lo)
+        if batch:
+            arrived(part_b.at[slots, 0], f"b1_{batch}")
         for i in (1, 2, 3):
-            b = back_y(i)
-            b2.append(
-                send(
-                    part_b.at[pl.ds(lo, hi - lo), 0], part_b.at[pl.ds(lo, hi - lo), b],
-                    sem_b2, 4 * batch + b, to_y(i),
-                )
-            )
+            send(part_b.at[slots, 0], part_b.at[slots, back_y(i)], "b2", f"b2_{batch}", to_y(i))
 
     def spread_arrived(batch):
         lo, hi = Z_BATCHES[batch]
-        for i in (1, 2, 3):
-            arrived(part_b.at[pl.ds(lo, hi - lo), i], sem_b2, 4 * batch + i)
+        arrived(part_b.at[pl.ds(lo, hi - lo), pl.ds(1, NY - 1)], f"b2_{batch}")
 
     def project(part, total, slot, dz, columns):
         at = pl.multiple_of((z + dz) % NZ * 256, 256)
@@ -346,7 +341,7 @@
 
     spread(0)
     for i in (1, 2, 3):
-        arrived(part_a.at[0, i], sem_a1, i)
+        arrived(part_a.at[0, i], f"a1_{i}")
         give(0, i, (1, -1, 2, -2))
         if i == 2:
             spread(1)
@@ -354,21 +349,55 @@
     get_w.wait()
     project_a((0,), 0)
     for i in range(NY):
-        got(6, i)
+        arrived(part_a.at[pl.ds(0, 2), i], f"a2_{i}")
         give(6, i, (1, 2))
-        got(2, i)
         give(2, i, (-1, -2))
-        if i == 0:
-            spread(3)
-        got(1, i)
-        got(7, i)
+        if i < 2:
+            spread(3 + i)
+    arrived(part_a.at[pl.ds(0, 2)], "a2_side")
     project_a((1, 7, 2, 6), 0)
     for batch in range(3):
         spread_arrived(batch)
         project_b((batch,), 0)
 
-    for cp in tt_copies:
-        cp.wait()
+    arrived(w_all.at[1], "w")
+    project_a((0, 1, 7, 2, 6), 1)
+    project_b((0, 1, 2), 1)
+
+    def rows_of(head, size):
+        dy = (head + NY - y) % NY
+        return pl.ds(pl.multiple_of(size * jnp.where(dy >= 2, 5 - dy, dy), size), size)
+
+    def share(total, sent, got, name, size):
+        for columns, d in ((0, 2), (1, 2), (0, 3), (1, 3), (0, 1), (1, 1), (1, 0)):
+            slot = NH * columns + d
+            back = NH * columns + (NH - d) % NH
+            sent[slot] = total[columns, rows_of((h + d) % NH, size)].astype(BF16)
+            send(sent.at[slot], got.at[back], name, name, dev(dx=columns, dh=d))
+
+    def finish(total, got, name, first, size):
+        arrived(got.at[pl.ds(1, 2 * NH - 1)], name)
+        whole = [total[0, rows_of(h, size)], got[NH].astype(F32)]
+        for columns in range(2):
+            for d in range(1, NH):
+                whole[columns] = whole[columns] + got[NH * columns + d].astype(F32)
+            for j in range(size // ROWS):
+                at = 16 * (first + j) + 8 * ((x + columns) % NX)
+                out_ref[pl.ds(pl.multiple_of(at, 8), 8)] = whole[columns][8 * j : 8 * j + 8]
+        rows = pl.ds(16 * first, 2 * size)
+        outs.append(put(out_ref.at[rows], out_hbm.at[rows], 2 + (first > 0)))
+
+    for batch in (3, 4):
+        spread_arrived(batch)
+    project_b((3, 4), 0)
+    project_b((3, 4), 1)
+    share(sum_b, hb_send, hb_recv, "hb", RB)
+    arrived(part_a.at[pl.ds(3, 3)], "a2_far")
+    project_a((3, 5, 4), 0)
+    project_a((3, 5, 4), 1)
+    share(sum_a, ha_send, ha_recv, "ha", RA)
+
+    arrived(turn_all.at[:, pl.ds(1, NYX - 1)], "tt")
     col = iota((128, 1024), 1)
     of_piece = 32 * (col // 32 % 4) + 4 * (col // 128) + 2 * (col // 16 % 2) + col // 4 % 2
     slot_of = mm(
@@ -381,52 +410,28 @@
     kind = col // 8 % 2
     ak_ref[...] = mm((chosen & (kind == 0)).astype(BF16), every).astype(BF16)
     av_ref[...] = mm((chosen & (kind == 1)).astype(BF16), every).astype(BF16)
-
-    for cp in w_copies:
+    outs = [put(ak_ref, ak_hbm, 0), put(av_ref, av_hbm, 1)]
+
+    finish(sum_b, hb_recv, "hb", NA, RB)
+    left(q_all.at[others], "q")
+    left(k_all.at[others], "k")
+    left(v_all.at[others], "v")
+    left(turn_yx.at[others], "t")
+    left(turn_yx.at[others], "tz")
+    left(turn_all.at[others], "tt")
+    left(st_recv.at[others], "st")
+    for half in range(2):
+        left(o_recv.at[others, halves[half]], f"rs{half}")
+    left(part_a.at[0, pl.ds(1, NY - 1)], "a1")
+    left(part_b.at[others, 0], "b1")
+    left(part_a.at[others], "a2")
+    left(part_b.at[:, pl.ds(1, NY - 1)], "b2")
+    left(w_all.at[1], "w")
+    left(hb_send.at[others], "hb")
+    finish(sum_a, ha_recv, "ha", 0, RA)
+    left(ha_send.at[others], "ha")
+    for cp in outs:
         cp.wait()
-    project_a((0, 1, 7, 2, 6), 1)
-    project_b((0, 1, 2), 1)
-
-    def rows_of(head, size):
-        dy = (head + NY - y) % NY
-        return pl.ds(pl.multiple_of(size * jnp.where(dy >= 2, 5 - dy, dy), size), size)
-
-    def share(total, sent, got, base, size):
-        copies = []
-        for columns, d in ((0, 2), (1, 2), (0, 3), (1, 3), (0, 1), (1, 1), (1, 0)):
-            slot = NH * columns + d
-            back = NH * columns + (NH - d) % NH
-            sent[slot] = total[columns, rows_of((h + d) % NH, size)].astype(BF16)
-            copies.append(
-                send(sent.at[slot], got.at[back], sem_h, base + back, dev(dx=columns, dh=d))
-            )
-        return copies
-
-    def finish(total, got, copies, first, size):
-        for cp in copies:
-            cp.wait()
-        whole = [total[0, rows_of(h, size)], got[NH].astype(F32)]
-        for columns in range(2):
-            for d in range(1, NH):
-                whole[columns] = whole[columns] + got[NH * columns + d].astype(F32)
-            for j in range(size // ROWS):
-                at = 16 * (first + j) + 8 * ((x + columns) % NX)
-                out_ref[pl.ds(pl.multiple_of(at, 8), 8)] = whole[columns][8 * j : 8 * j + 8]
-
-    spread_arrived(3)
-    project_b((3,), 0)
-    project_b((3,), 1)
-    to_b = share(sum_b, hb_send, hb_recv, 0, RB)
-    for slot in (3, 5, 4):
-        for i in range(NY):
-            got(slot, i)
-        project_a((slot,), 0)
-        project_a((slot,), 1)
-    to_a = share(sum_a, ha_send, ha_recv, 8, RA)
-    finish(sum_b, hb_recv, to_b, NA, RB)
-    for cp in kv_copies + list(q_copies.values()) + a1 + b1 + b2 + a2:
-        cp.wait_send()
-    finish(sum_a, ha_recv, to_a, 0, RA)
 
 
 def write_out(a_in, b_in, c_in, a_out, b_out, c_out, a_mid, b_mid, c_mid, sems):
@@ -448,8 +453,6 @@
     block_mask, doc_ids, slot_ids, out_weight,
 ):
     anywhere = pl.BlockSpec(memory_space=pl.ANY)
-    vmem = pl.BlockSpec(memory_space=pltpu.VMEM)
-    sems = lambda n: pltpu.SemaphoreType.DMA((2, n))
     results = pl.pallas_call(
         kernel,
         out_shape=(
@@ -458,7 +461,7 @@
             jax.ShapeDtypeStruct((16, HEAD), BF16),
         ),
         in_specs=[anywhere] * 9,
-        out_specs=(vmem, vmem, vmem),
+        out_specs=(anywhere,) * 3,
         scratch_shapes=[
             pltpu.VMEM((128, HEAD), BF16),
             pltpu.VMEM((NZ, 128, HEAD), BF16),
@@ -480,6 +483,8 @@
             pltpu.VMEM((NZ, NZ, 16, HEAD), BF16),
             pltpu.VMEM((NZ, 2 * NZ, 128), F32),
             pltpu.VMEM((128, 128), F32),
+            pltpu.VMEM((NZ * NZ, 16, HEAD), F32),
+            pltpu.VMEM((NZ, 128, 128), F32),
             pltpu.VMEM((NZ, NY, RA, 256), BF16),
             pltpu.VMEM((NZ, NY, RB, 256), BF16),
             pltpu.VMEM((NX, NY * RA, 256), F32),
@@ -488,9 +493,13 @@
             pltpu.VMEM((2 * NH, RA, 256), BF16),
             pltpu.VMEM((2 * NH, RB, 256), BF16),
             pltpu.VMEM((2 * NH, RB, 256), BF16),
+            pltpu.VMEM((128, 256), F32),
+            pltpu.VMEM((16, HEAD), BF16),
+            pltpu.VMEM((16, HEAD), BF16),
             pltpu.SemaphoreType.DMA((9,)),
-            sems(W_PARTS), sems(8), sems(16), sems(8), sems(8), sems(8), sems(24), sems(4), sems(8), sems(32),
-            sems(16), sems(16),
+            pltpu.SemaphoreType.DMA((4,)),
+            pltpu.SemaphoreType.DMA((len(SENT),)),
+            pltpu.SemaphoreType.DMA((len(GOT),)),
         ],
         compiler_params=pltpu.CompilerParams(
             collective_id=0, has_side_effects=True, vmem_limit_bytes=60 * 1024 * 1024

time: 57.9 us -> 54.7 us (0.945)
  Pallas kernels: 57.1 us -> 54 us
    pallas_call x1, Pallas kernels: 55.5 us -> 52.3 us  [on_device(): pl.pallas_call(kernel, out_shape=(jax.ShapeDtypeStruct((128, 256), F32),...]
where the time goes in v5:
time: 54.7 us; the launch traced here: 54.6 us
  Pallas kernels  54 us (99%)
  between operations  0.64 us (1%)
    pallas_call x1, Pallas kernels, on_device(): pl.pallas_call(kernel, out_shape=(jax.ShapeDtypeStruct((128, 256), F32),...  52.3 us
    pallas_call x1, Pallas kernels, on_device(): pl.pallas_call(write_out, out_shape=tuple((jax.ShapeDtypeStruct(r.shape,...  1.62 us

profile of v5, /device:TPU:1, one launch (start us, length us, event | category | flops | bytes accessed | tf_op | source)
XLA Modules:
  0.0 54.6 jit_solution(8839609222356179746)
XLA Ops:
  0.6 52.3 %turn_attention.1 = (f32[128,256]{1,0:T(8,128)}, bf16[16,128]{1,0:T(8,128)(2,1)}, bf16[16,128]{1,0:T(8,128)(2,1)}) custom-call(bf16[128,128]{1,0:T(8,128)(2,1)} %bitcast.11, bf16[256,128]{1,0:T(8,128)(2,1)} %bitcast.9, bf16[256,128]{1,0:T(8,128)(2,1)} %bitcast.10, bf16[2048,256]{1,0:T(8,128)(2,1)} %w_in.1, bf16[8,128]{1,0:T(8,128)(2,1)} %bitcast.12, ...), custom_call_target="tpu_custom_call" | custom-call | tf_op jit(solution)/shard_map/turn_attention/pallas_call | solution.py:456
  53.0 1.6 %write_out.1 = (f32[128,256]{1,0:T(8,128)}, bf16[16,128]{1,0:T(8,128)(2,1)}, bf16[16,128]{1,0:T(8,128)(2,1)}) custom-call(f32[128,256]{1,0:T(8,128)} %get-tuple-element.9.a_in, bf16[16,128]{1,0:T(8,128)(2,1)} %get-tuple-element.10.b_in, bf16[16,128]{1,0:T(8,128)(2,1)} %get-tuple-element.11.c_in), custom_call_target="tpu_custom_call" | custom-call | tf_op jit(solution)/shard_map/write_out/pallas_call | solution.py:519

commit v6 on v5

--- a/solution.py
+++ b/solution.py
@@ -32,11 +32,11 @@
 RA, RB = NA * ROWS, (NZ - NA) * ROWS
 DIRECT = True
 SENT = [
-    "q", "k", "v", "t", "tz", "tt", "st", "rs0", "rs1", "a1", "b1", "a2", "b2", "ha", "hb", "w",
+    "q", "k", "v", "t", "tz", "tt", "st", "rs", "a1", "b1", "a2", "b2", "ha", "hb", "w",
 ]
 GOT = [
     "q0", "q1", "q2", "q3", "v1", "k1", "k2", "k4", "k6", "g1", "g2", "g3", "t", "tz", "tt", "st",
-    "rs0", "rs1", "a1_1", "a1_2", "a1_3", "b1_1", "b1_2", "b1_3", "b1_4", "a2_0", "a2_1", "a2_2",
+    "rs", "a1_1", "a1_2", "a1_3", "b1_1", "b1_2", "b1_3", "b1_4", "a2_0", "a2_1", "a2_2",
     "a2_3", "a2_side", "a2_far", "b2_0", "b2_1", "b2_2", "b2_3", "b2_4", "ha", "hb", "w",
 ]
 KEY_GROUPS = [(0, 1), (2, 4), (6, 3), (5, 7)]
@@ -56,6 +56,10 @@
 
 def iota(shape, dim):
     return lax.broadcasted_iota(jnp.int32, shape, dim)
+
+
+def around(i, step, size):
+    return lax.rem(i + step % size, size) if step % size else i
 
 
 def back_yx(r):
@@ -73,12 +77,12 @@
 ):
     c = lax.axis_index("ctx")
     h = lax.axis_index("head")
-    y, z, x = c // (NZ * NX), (c // NX) % NZ, c % NX
+    y, z, x = lax.div(c, NZ * NX), lax.rem(lax.div(c, NX), NZ), lax.rem(c, NX)
     yx = y * NX + x
 
     def dev(dy=0, dz=0, dx=0, dh=0):
-        ty, tz, tx = (y + dy) % NY, (z + dz) % NZ, (x + dx) % NX
-        return ((ty * NZ + tz) * NX + tx, (h + dh) % NH)
+        ty, tz, tx = around(y, dy, NY), around(z, dz, NZ), around(x, dx, NX)
+        return ((ty * NZ + tz) * NX + tx, around(h, dh, NH))
 
     def to_y(i):
         return dev(dy=YS[i])
@@ -174,7 +178,7 @@
     right_key = (i1 // 8 % 2 == 0)
 
     def sight(slot):
-        query_token = 16 * ((z + ZS[slot]) % NZ) + 8 * x + i0 % 8
+        query_token = 16 * around(z, ZS[slot], NZ) + 8 * x + i0 % 8
         query_doc = jnp.sum(jnp.where(i1 == query_token, doc_mine, 0.0), axis=1, keepdims=True)
         see = (
             (128 * (i1 // 32) + key_token <= 128 * y + query_token)
@@ -210,10 +214,10 @@
             v_wide[g, :, HEAD:] = jnp.ones((2 * KEYS, HEAD), BF16)
             biases[g] = []
             for r in KEY_GROUPS[g]:
-                source = ((y + YX[r][0]) % NY * NZ + z) * NX + (x + YX[r][1]) % NX
+                source = (around(y, YX[r][0], NY) * NZ + z) * NX + around(x, YX[r][1], NX)
                 for b in range(2):
                     biases[g].append(jnp.where(mask_ref[y, 2 * source + b] == 1, 0.0, NEG))
-            if g == 1:
+            if last:
                 arrived(turn_yx.at[pl.ds(1, NYX - 1)], "t")
                 fresh = turn_yx[...].reshape(128, HEAD)
                 fresh_v = mm((i1 == i0 + 8).astype(BF16), fresh).astype(BF16)
@@ -228,7 +232,7 @@
                 s[:, :128] * SCALE + biases[g][2 * j], s[:, 128:] * SCALE + biases[g][2 * j + 1]
             ]
         values = v_wide[g]
-        if g == 1:
+        if last:
             parts.append(nt(q, fresh) * SCALE + sights[2 * i : 2 * i + 2].reshape(256, 128))
             values = jnp.concatenate([values, fresh_v], axis=0)
         top = parts[0]
@@ -248,7 +252,7 @@
             continue
         for j in range(2):
             rows = slice(128 * j, 128 * (j + 1))
-            of = (z + ZS[2 * i + j]) % NZ
+            of = around(z, ZS[2 * i + j], NZ)
             o_send[:, of] = o[rows, :HEAD].astype(BF16).reshape(NZ, 16, HEAD)
             st_send[pl.ds(of, 1)] = jnp.sum(
                 jnp.where(diagonal, top[rows], 0.0), axis=0, keepdims=True
@@ -257,15 +261,10 @@
                 jnp.where(diagonal, o[rows, HEAD:], 0.0), axis=0, keepdims=True
             )
 
-    halves = (pl.ds(0, NA), pl.ds(NA, NZ - NA))
     for d in Z_ORDER:
         send(st_send, st_recv.at[z], "st", "st", dev(dz=d))
-    for half in range(2):
-        for d in Z_ORDER:
-            send(
-                o_send.at[(z + d) % NZ, halves[half]], o_recv.at[z, halves[half]],
-                f"rs{half}", f"rs{half}", dev(dz=d),
-            )
+    for d in (4, 3, 5, 2, 6, 1, 7):
+        send(o_send.at[around(z, d, NZ)], o_recv.at[z], "rs", "rs", dev(dz=d))
     o_recv[z] = o_send[z]
     st_recv[z] = st_send[...]
     others = pl.ds(1, NZ - 1)
@@ -292,7 +291,7 @@
             out.append(jnp.concatenate([num[:ROWS], num[ROWS:]], axis=1))
         return jnp.concatenate(out, axis=0).astype(BF16)
 
-    arrived(o_recv.at[others, halves[0]], "rs0")
+    arrived(o_recv.at[others], "rs")
     part_a[0, 0] = attended(0)
     for i in (1, 2, 3):
         send(part_a.at[0, 0], part_a.at[0, back_y(i)], "a1", f"a1_{back_y(i)}", to_y(i))
@@ -305,7 +304,6 @@
                 send(part_a.at[slot, i], part_a.at[dst, i], "a2", got, dev(dz=step))
 
     give(0, 0, (1, -1, 2, -2))
-    arrived(o_recv.at[others, halves[1]], "rs1")
     part_b[0, 0] = attended(1)
     batch_of = {s: k for k, (lo, hi) in enumerate(Z_BATCHES) for s in range(lo, hi)}
     for d in Z_ORDER:
@@ -325,7 +323,7 @@
         arrived(part_b.at[pl.ds(lo, hi - lo), pl.ds(1, NY - 1)], f"b2_{batch}")
 
     def project(part, total, slot, dz, columns):
-        at = pl.multiple_of((z + dz) % NZ * 256, 256)
+        at = pl.multiple_of(around(z, dz, NZ) * 256, 256)
         size = part.shape[1] * part.shape[2]
         new = mm(part[slot].reshape(size, 256), w_all[columns, pl.ds(at, 256)])
         total[columns] = new if dz == 0 else total[columns] + new
@@ -365,14 +363,14 @@
     project_b((0, 1, 2), 1)
 
     def rows_of(head, size):
-        dy = (head + NY - y) % NY
+        dy = lax.rem(head + NY - y, NY)
         return pl.ds(pl.multiple_of(size * jnp.where(dy >= 2, 5 - dy, dy), size), size)
 
     def share(total, sent, got, name, size):
         for columns, d in ((0, 2), (1, 2), (0, 3), (1, 3), (0, 1), (1, 1), (1, 0)):
             slot = NH * columns + d
             back = NH * columns + (NH - d) % NH
-            sent[slot] = total[columns, rows_of((h + d) % NH, size)].astype(BF16)
+            sent[slot] = total[columns, rows_of(around(h, d, NH), size)].astype(BF16)
             send(sent.at[slot], got.at[back], name, name, dev(dx=columns, dh=d))
 
     def finish(total, got, name, first, size):
@@ -382,7 +380,7 @@
             for d in range(1, NH):
                 whole[columns] = whole[columns] + got[NH * columns + d].astype(F32)
             for j in range(size // ROWS):
-                at = 16 * (first + j) + 8 * ((x + columns) % NX)
+                at = 16 * (first + j) + 8 * around(x, columns, NX)
                 out_ref[pl.ds(pl.multiple_of(at, 8), 8)] = whole[columns][8 * j : 8 * j + 8]
         rows = pl.ds(16 * first, 2 * size)
         outs.append(put(out_ref.at[rows], out_hbm.at[rows], 2 + (first > 0)))
@@ -420,8 +418,7 @@
     left(turn_yx.at[others], "tz")
     left(turn_all.at[others], "tt")
     left(st_recv.at[others], "st")
-    for half in range(2):
-        left(o_recv.at[others, halves[half]], f"rs{half}")
+    left(o_recv.at[others], "rs")
     left(part_a.at[0, pl.ds(1, NY - 1)], "a1")
     left(part_b.at[others, 0], "b1")
     left(part_a.at[others], "a2")

time: 54.7 us -> 53.3 us (0.974)
  Pallas kernels: 54 us -> 52.5 us
    pallas_call x1, Pallas kernels: 52.3 us -> 50.9 us  [on_device(): pl.pallas_call(kernel, out_shape=(jax.ShapeDtypeStruct((128, 256), F32),...]
where the time goes in v6:
time: 53.3 us; the launch traced here: 53.2 us
  Pallas kernels  52.5 us (98%)
  between operations  0.64 us (1%)
    pallas_call x1, Pallas kernels, on_device(): pl.pallas_call(kernel, out_shape=(jax.ShapeDtypeStruct((128, 256), F32),...  50.9 us
    pallas_call x1, Pallas kernels, on_device(): pl.pallas_call(write_out, out_shape=tuple((jax.ShapeDtypeStruct(r.shape,...  1.62 us

profile of v6, /device:TPU:1, one launch (start us, length us, event | category | flops | bytes accessed | tf_op | source)
XLA Modules:
  0.0 53.2 jit_solution(15165964778343302044)
XLA Ops:
  0.6 50.9 %turn_attention.1 = (f32[128,256]{1,0:T(8,128)}, bf16[16,128]{1,0:T(8,128)(2,1)}, bf16[16,128]{1,0:T(8,128)(2,1)}) custom-call(bf16[128,128]{1,0:T(8,128)(2,1)} %bitcast.11, bf16[256,128]{1,0:T(8,128)(2,1)} %bitcast.9, bf16[256,128]{1,0:T(8,128)(2,1)} %bitcast.10, bf16[2048,256]{1,0:T(8,128)(2,1)} %w_in.1, bf16[8,128]{1,0:T(8,128)(2,1)} %bitcast.12, ...), custom_call_target="tpu_custom_call" | custom-call | tf_op jit(solution)/shard_map/turn_attention/pallas_call | solution.py:453
  51.6 1.6 %write_out.1 = (f32[128,256]{1,0:T(8,128)}, bf16[16,128]{1,0:T(8,128)(2,1)}, bf16[16,128]{1,0:T(8,128)(2,1)}) custom-call(f32[128,256]{1,0:T(8,128)} %get-tuple-element.9.a_in, bf16[16,128]{1,0:T(8,128)(2,1)} %get-tuple-element.10.b_in, bf16[16,128]{1,0:T(8,128)(2,1)} %get-tuple-element.11.c_in), custom_call_target="tpu_custom_call" | custom-call | tf_op jit(solution)/shard_map/write_out/pallas_call | solution.py:516

commit v7 on v6

--- a/solution.py
+++ b/solution.py
@@ -340,7 +340,7 @@
     spread(0)
     for i in (1, 2, 3):
         arrived(part_a.at[0, i], f"a1_{i}")
-        give(0, i, (1, -1, 2, -2))
+        give(0, i, (4, -4, 3, -3, 2, -2, 1, -1) if i == 3 else (1, -1, 2, -2))
         if i == 2:
             spread(1)
     spread(2)
@@ -348,8 +348,9 @@
     project_a((0,), 0)
     for i in range(NY):
         arrived(part_a.at[pl.ds(0, 2), i], f"a2_{i}")
-        give(6, i, (1, 2))
-        give(2, i, (-1, -2))
+        if not (i == 3):
+            give(6, i, (1, 2))
+            give(2, i, (-1, -2))
         if i < 2:
             spread(3 + i)
     arrived(part_a.at[pl.ds(0, 2)], "a2_side")

time: 53.3 us -> 53.3 us (level)
  no operation moved by 1% of the time
where the time goes in v7:
time: 53.3 us; the launch traced here: 53.2 us
  Pallas kernels  52.5 us (98%)
  between operations  0.64 us (1%)
    pallas_call x1, Pallas kernels, on_device(): pl.pallas_call(kernel, out_shape=(jax.ShapeDtypeStruct((128, 256), F32),...  50.9 us
    pallas_call x1, Pallas kernels, on_device(): pl.pallas_call(write_out, out_shape=tuple((jax.ShapeDtypeStruct(r.shape,...  1.62 us

profile of v7, /device:TPU:1, one launch (start us, length us, event | category | flops | bytes accessed | tf_op | source)
XLA Modules:
  0.0 53.2 jit_solution(8755692919349922933)
XLA Ops:
  0.6 50.9 %turn_attention.1 = (f32[128,256]{1,0:T(8,128)}, bf16[16,128]{1,0:T(8,128)(2,1)}, bf16[16,128]{1,0:T(8,128)(2,1)}) custom-call(bf16[128,128]{1,0:T(8,128)(2,1)} %bitcast.11, bf16[256,128]{1,0:T(8,128)(2,1)} %bitcast.9, bf16[256,128]{1,0:T(8,128)(2,1)} %bitcast.10, bf16[2048,256]{1,0:T(8,128)(2,1)} %w_in.1, bf16[8,128]{1,0:T(8,128)(2,1)} %bitcast.12, ...), custom_call_target="tpu_custom_call" | custom-call | tf_op jit(solution)/shard_map/turn_attention/pallas_call | solution.py:454
  51.6 1.6 %write_out.1 = (f32[128,256]{1,0:T(8,128)}, bf16[16,128]{1,0:T(8,128)(2,1)}, bf16[16,128]{1,0:T(8,128)(2,1)}) custom-call(f32[128,256]{1,0:T(8,128)} %get-tuple-element.9.a_in, bf16[16,128]{1,0:T(8,128)(2,1)} %get-tuple-element.10.b_in, bf16[16,128]{1,0:T(8,128)(2,1)} %get-tuple-element.11.c_in), custom_call_target="tpu_custom_call" | custom-call | tf_op jit(solution)/shard_map/write_out/pallas_call | solution.py:517

commit v8 on v6

--- a/solution.py
+++ b/solution.py
@@ -31,9 +31,6 @@
 NA = 4
 RA, RB = NA * ROWS, (NZ - NA) * ROWS
 DIRECT = True
-SENT = [
-    "q", "k", "v", "t", "tz", "tt", "st", "rs", "a1", "b1", "a2", "b2", "ha", "hb", "w",
-]
 GOT = [
     "q0", "q1", "q2", "q3", "v1", "k1", "k2", "k4", "k6", "g1", "g2", "g3", "t", "tz", "tt", "st",
     "rs", "a1_1", "a1_2", "a1_3", "b1_1", "b1_2", "b1_3", "b1_4", "a2_0", "a2_1", "a2_2",
@@ -93,9 +90,10 @@
     def to_yx(r):
         return dev(dy=YX[r][0], dx=YX[r][1])
 
-    def send(src, dst, sent, got, device):
+    def send(src, dst, got, device):
+        sent = 2 if got == "ha" else (0 if got[0] in "kvgw" else 1)
         pltpu.make_async_remote_copy(
-            src_ref=src, dst_ref=dst, send_sem=sem_sent.at[SENT.index(sent)],
+            src_ref=src, dst_ref=dst, send_sem=sem_sent.at[sent],
             recv_sem=sem_got.at[GOT.index(got)], device_id=device, device_id_type=MESH,
         ).start()
 
@@ -103,7 +101,7 @@
         pltpu.make_async_copy(ref, ref, sem_got.at[GOT.index(got)]).wait()
 
     def left(ref, sent):
-        pltpu.make_async_copy(ref, ref, sem_sent.at[SENT.index(sent)]).wait()
+        pltpu.make_async_copy(ref, ref, sem_sent.at[sent]).wait()
 
     def put(src, dst, i):
         copy = pltpu.make_async_copy(src, dst, sem_out.at[i])
@@ -116,8 +114,9 @@
         return copy
 
     barrier = pltpu.get_barrier_semaphore()
-    peers = [to_yx(r) for r in YX_ORDER] + [dev(dz=d) for d in Z_ORDER]
+    peers = [dev(dz=d) for d in (4, 3, 5, 2, 6)] + [to_yx(r) for r in (7, 6, 5, 3)]
     peers += [dev(dx=dx, dh=d) for dx in range(NX) for d in range(1, NH)]
+    peers += [to_yx(r) for r in (4, 2, 1)] + [dev(dz=d) for d in (1, 7)]
     for p in peers:
         pl.semaphore_signal(barrier, inc=1, device_id=p, device_id_type=MESH)
 
@@ -133,11 +132,11 @@
 
     def give_k(src, slot, device):
         got = f"k{slot}" if slot in (1, 2, 4, 6) else ("g2" if slot == 3 else "g3")
-        send(src, k_all.at[slot], "k", got, device)
+        send(src, k_all.at[slot], got, device)
 
     def give_v(src, slot, device):
         got = {1: "v1", 2: "g1", 4: "g1", 3: "g2", 6: "g2"}.get(slot, "g3")
-        send(src, v_all.at[slot], "v", got, device)
+        send(src, v_all.at[slot], got, device)
 
     give_v(cv_in, 1, to_yx(1))
     for r in (2, 4, 6):
@@ -152,16 +151,16 @@
     q_all[0] = mm(order, q_raw[...]).astype(BF16)
     for d in Z_ORDER:
         slot = ZS.index(NZ - d)
-        send(q_all.at[0], q_all.at[slot], "q", f"q{slot // 2}", dev(dz=d))
+        send(q_all.at[0], q_all.at[slot], f"q{slot // 2}", dev(dz=d))
     for cp in get_small:
         cp.wait()
     mine = jnp.concatenate([tk[...].astype(F32), tv[...].astype(F32)], axis=0).astype(BF16)
     turn_yx[yx] = mine
     turn_all[z, yx] = mine
     for r in YX_ORDER:
-        send(turn_yx.at[yx], turn_yx.at[yx], "t", "t", to_yx(r))
+        send(turn_yx.at[yx], turn_yx.at[yx], "t", to_yx(r))
     for d in Z_ORDER:
-        send(turn_yx.at[yx], turn_all.at[z, yx], "tz", "tz", dev(dz=d))
+        send(turn_yx.at[yx], turn_all.at[z, yx], "tz", dev(dz=d))
 
     docs = docs_ref[...]
     key_token = 16 * z + 8 * (i1 // 16 % 2) + i1 % 8
@@ -197,7 +196,7 @@
     for r in (2, 4, 6):
         arrived(k_all.at[r], f"k{r}")
         give_k(k_all.at[r], r + 1, to_yx(1))
-    send(w_in, w_all.at[1], "w", "w", dev(dx=1))
+    send(w_in, w_all.at[1], "w", dev(dx=1))
 
     biases = {}
     for g, i in BLOCKS:
@@ -262,15 +261,15 @@
             )
 
     for d in Z_ORDER:
-        send(st_send, st_recv.at[z], "st", "st", dev(dz=d))
+        send(st_send, st_recv.at[z], "st", dev(dz=d))
     for d in (4, 3, 5, 2, 6, 1, 7):
-        send(o_send.at[around(z, d, NZ)], o_recv.at[z], "rs", "rs", dev(dz=d))
+        send(o_send.at[around(z, d, NZ)], o_recv.at[z], "rs", dev(dz=d))
     o_recv[z] = o_send[z]
     st_recv[z] = st_send[...]
     others = pl.ds(1, NZ - 1)
     arrived(turn_all.at[others, 0], "tz")
     for r in YX_ORDER:
-        send(turn_all.at[:, yx], turn_all.at[:, yx], "tt", "tt", to_yx(r))
+        send(turn_all.at[:, yx], turn_all.at[:, yx], "tt", to_yx(r))
     arrived(st_recv.at[others], "st")
     peaks, totals = st_recv[:, :NZ], st_recv[:, NZ:]
     factor = jnp.exp2(peaks - jnp.max(peaks, axis=0, keepdims=True))
@@ -294,21 +293,21 @@
     arrived(o_recv.at[others], "rs")
     part_a[0, 0] = attended(0)
     for i in (1, 2, 3):
-        send(part_a.at[0, 0], part_a.at[0, back_y(i)], "a1", f"a1_{back_y(i)}", to_y(i))
+        send(part_a.at[0, 0], part_a.at[0, back_y(i)], f"a1_{back_y(i)}", to_y(i))
 
     def give(slot, i, steps):
         for step in steps:
             dst = (slot - step) % NZ
             if dst != 4 or (step > 0) == (i < NY // 2):
                 got = f"a2_{i}" if dst in (2, 6) else ("a2_side" if dst in (1, 7) else "a2_far")
-                send(part_a.at[slot, i], part_a.at[dst, i], "a2", got, dev(dz=step))
+                send(part_a.at[slot, i], part_a.at[dst, i], got, dev(dz=step))
 
     give(0, 0, (1, -1, 2, -2))
     part_b[0, 0] = attended(1)
     batch_of = {s: k for k, (lo, hi) in enumerate(Z_BATCHES) for s in range(lo, hi)}
     for d in Z_ORDER:
         slot = ZS.index(NZ - d)
-        send(part_b.at[0, 0], part_b.at[slot, 0], "b1", f"b1_{batch_of[slot]}", dev(dz=d))
+        send(part_b.at[0, 0], part_b.at[slot, 0], f"b1_{batch_of[slot]}", dev(dz=d))
 
     def spread(batch):
         lo, hi = Z_BATCHES[batch]
@@ -316,7 +315,7 @@
         if batch:
             arrived(part_b.at[slots, 0], f"b1_{batch}")
         for i in (1, 2, 3):
-            send(part_b.at[slots, 0], part_b.at[slots, back_y(i)], "b2", f"b2_{batch}", to_y(i))
+            send(part_b.at[slots, 0], part_b.at[slots, back_y(i)], f"b2_{batch}", to_y(i))
 
     def spread_arrived(batch):
         lo, hi = Z_BATCHES[batch]
@@ -371,7 +370,7 @@
             slot = NH * columns + d
             back = NH * columns + (NH - d) % NH
             sent[slot] = total[columns, rows_of(around(h, d, NH), size)].astype(BF16)
-            send(sent.at[slot], got.at[back], name, name, dev(dx=columns, dh=d))
+            send(sent.at[slot], got.at[back], name, dev(dx=columns, dh=d))
 
     def finish(total, got, name, first, size):
         arrived(got.at[pl.ds(1, 2 * NH - 1)], name)
@@ -411,22 +410,10 @@
     outs = [put(ak_ref, ak_hbm, 0), put(av_ref, av_hbm, 1)]
 
     finish(sum_b, hb_recv, "hb", NA, RB)
-    left(q_all.at[others], "q")
-    left(k_all.at[others], "k")
-    left(v_all.at[others], "v")
-    left(turn_yx.at[others], "t")
-    left(turn_yx.at[others], "tz")
-    left(turn_all.at[others], "tt")
-    left(st_recv.at[others], "st")
-    left(o_recv.at[others], "rs")
-    left(part_a.at[0, pl.ds(1, NY - 1)], "a1")
-    left(part_b.at[others, 0], "b1")
-    left(part_a.at[others], "a2")
-    left(part_b.at[:, pl.ds(1, NY - 1)], "b2")
-    left(w_all.at[1], "w")
-    left(hb_send.at[others], "hb")
+    left(w_all.at[:, pl.ds(0, 1024 + 2 * 448)], 0)
+    left(w_all.at[:, pl.ds(0, 2 * 224 + 2 * 28 + 56 + 224 + 48 + 112 + 448 + 384 + 112)], 1)
     finish(sum_a, ha_recv, "ha", 0, RA)
-    left(ha_send.at[others], "ha")
+    left(ha_send.at[others], 2)
     for cp in outs:
         cp.wait()
 
@@ -495,7 +482,7 @@
             pltpu.VMEM((16, HEAD), BF16),
             pltpu.SemaphoreType.DMA((9,)),
             pltpu.SemaphoreType.DMA((4,)),
-            pltpu.SemaphoreType.DMA((len(SENT),)),
+            pltpu.SemaphoreType.DMA((3,)),
             pltpu.SemaphoreType.DMA((len(GOT),)),
         ],
         compiler_params=pltpu.CompilerParams(

time: 53.3 us -> 52.7 us (0.989)
    pallas_call x1, Pallas kernels: 50.9 us -> 50.4 us  [on_device(): pl.pallas_call(kernel, out_shape=(jax.ShapeDtypeStruct((128, 256), F32),...]
where the time goes in v8:
time: 52.7 us; the launch traced here: 52.6 us
  Pallas kernels  52 us (99%)
  between operations  0.64 us (1%)
    pallas_call x1, Pallas kernels, on_device(): pl.pallas_call(kernel, out_shape=(jax.ShapeDtypeStruct((128, 256), F32),...  50.4 us
    pallas_call x1, Pallas kernels, on_device(): pl.pallas_call(write_out, out_shape=tuple((jax.ShapeDtypeStruct(r.shape,...  1.62 us

profile of v8, /device:TPU:1, one launch (start us, length us, event | category | flops | bytes accessed | tf_op | source)
XLA Modules:
  0.0 52.6 jit_solution(13360586063354067233)
XLA Ops:
  0.6 50.4 %turn_attention.1 = (f32[128,256]{1,0:T(8,128)}, bf16[16,128]{1,0:T(8,128)(2,1)}, bf16[16,128]{1,0:T(8,128)(2,1)}) custom-call(bf16[128,128]{1,0:T(8,128)(2,1)} %bitcast.11, bf16[256,128]{1,0:T(8,128)(2,1)} %bitcast.9, bf16[256,128]{1,0:T(8,128)(2,1)} %bitcast.10, bf16[2048,256]{1,0:T(8,128)(2,1)} %w_in.1, bf16[8,128]{1,0:T(8,128)(2,1)} %bitcast.12, ...), custom_call_target="tpu_custom_call" | custom-call | tf_op jit(solution)/shard_map/turn_attention/pallas_call | solution.py:440
  51.0 1.6 %write_out.1 = (f32[128,256]{1,0:T(8,128)}, bf16[16,128]{1,0:T(8,128)(2,1)}, bf16[16,128]{1,0:T(8,128)(2,1)}) custom-call(f32[128,256]{1,0:T(8,128)} %get-tuple-element.9.a_in, bf16[16,128]{1,0:T(8,128)(2,1)} %get-tuple-element.10.b_in, bf16[16,128]{1,0:T(8,128)(2,1)} %get-tuple-element.11.c_in), custom_call_target="tpu_custom_call" | custom-call | tf_op jit(solution)/shard_map/write_out/pallas_call | solution.py:503
